TPU v7x, 128 devices: a whole 4x4x4 slice. The times are simulated.
128 devices in a mesh: vol: 2 (over core), wide: 32 (over z_hi, x, y), narrow: 2 (over z_lo).
Axes of the slice: x: 4, y: 4, z: 4 (z_hi: 2, z_lo: 2; z = z_hi * 2 + z_lo), core: 2. Of those that a mesh axis runs over, the one named last changes fastest.
Arguments:
- forcing: float32 [2, 4, 384, 4096], P(None, 'vol', 'narrow', 'wide'), may hold values from -180 to 180
- material_ids: int32 [4, 384, 4096], P('vol', 'narrow', 'wide'), may hold values from 0 to 7
- materials: float32 [8], replicated, may hold values from 0.5 to 2
- boundary_operator: bfloat16 [4096, 131072], P('wide', 'narrow'), may hold values from -0.015625 to 0.015625
Outputs:
- pressure: float32 [2, 4, 384, 4096], P(None, 'vol', 'narrow', 'wide')
- traction: float32 [4096, 2], P(('wide', 'narrow'), 'vol')
All inputs are finite; a program needn't handle non-finite values.
Results may differ from a plain program's by a relative error of at most 0.0031.
Values may be sent and summed in bfloat16 or wider, within the bound.
A program may use at most 128 MiB of HBM per device.

v0:
```python
import jax
import jax.numpy as jnp
from jax import lax
from jax.sharding import PartitionSpec as P

BY = 16
RY = 1
RX = 64
MAT = 8
ITERS = 2


lower_edge = 0.25
upper_edge = 1.75
mass_ratio = 26.0
couple_gain = 40.0


def with_halo(shard, sides, width):
    for axis, dim in sides:
        peers, length = (lax.axis_size(axis), shard.shape[dim])
        up = [(i, (i + 1) % peers) for i in range(peers - 1)]
        down = [(j, i) for i, j in up]
        last = lax.slice_in_dim(shard, length - width, length, axis=dim)
        first = lax.slice_in_dim(shard, 0, width, axis=dim)
        before = lax.ppermute(last, axis, up)
        after = lax.ppermute(first, axis, down)
        shard = jnp.concatenate([before, shard, after], axis=dim)
    return shard


def from_root(shard, axis, root):
    mine = lax.axis_index(axis) == root
    return lax.psum(jnp.where(mine, shard, jnp.zeros_like(shard)), axis)


def sweep_weights():
    middle = (upper_edge + lower_edge) / 2.0
    spread = (upper_edge - lower_edge) / 2.0
    center_ratio = middle / spread
    ratio_last = 1.0 / center_ratio
    weights = [(0.0, 1.0 / middle)]
    ratio_next = 1.0 / (2.0 * center_ratio - ratio_last)
    weights.append((ratio_next * ratio_last, 2.0 * ratio_next / spread))
    return weights


def box_sum(padded):
    along = padded[..., :-2] + padded[..., 1:-1] + padded[..., 2:]
    along = along[..., :-2, :] + along[..., 1:-1, :] + along[..., 2:, :]
    return along[..., :-2, :, :] + along[..., 1:-1, :, :] + along[..., 2:, :, :]


def apply_operator(padded, center, cond_pad, conductance, diagonal):
    neighbours = box_sum(padded) - center
    weighted = box_sum(padded * cond_pad) - conductance * center
    return diagonal * center - 0.5 * (conductance * neighbours + weighted)


def relax(vol_field, source, cond_pad, conductance, diagonal):
    moved = jnp.zeros_like(vol_field)
    for keep_weight, gain_weight in sweep_weights():
        padded = with_halo(vol_field, (("vol", 1), ("wide", 3), ("narrow", 2)), 1)
        scaled = (
            source - apply_operator(padded, vol_field, cond_pad, conductance, diagonal)
        ) / diagonal
        moved = keep_weight * moved + gain_weight * scaled
        vol_field = vol_field + moved
    return vol_field


def fold_traces(mine, plane):
    return jnp.einsum(
        "ryx,kyx->rk",
        plane,
        lax.all_gather(mine, "wide", axis=2, tiled=True),
        preferred_element_type=jnp.float32,
    )


def local(forcing, material_ids, materials, boundary_operator):
    conductance = jnp.zeros(material_ids.shape, jnp.float32)
    for number in range(MAT):
        conductance = conductance + jnp.where(material_ids == number, materials[number], 0.0)
    cond_pad = with_halo(conductance, (("vol", 0), ("wide", 2), ("narrow", 1)), 1)
    diagonal = (
        0.5 * (26.0 * conductance + (box_sum(cond_pad) - conductance)) + mass_ratio * conductance
    )
    vol_count = lax.axis_size("vol")
    last_vol = vol_count - 1
    own_vol = lax.axis_index("vol")
    excite = forcing.shape[0]
    half_count = excite // vol_count
    tile_rows = boundary_operator.shape[0]
    cells_y = forcing.shape[2]
    cells_x = forcing.shape[3]
    stride = cells_y // BY
    plane = boundary_operator.reshape(tile_rows, BY, -1)
    is_top = (own_vol == last_vol).astype(jnp.float32)
    pressure = jnp.zeros(forcing.shape, jnp.float32)
    source = forcing
    traction = jnp.zeros((tile_rows // lax.axis_size("narrow"), half_count), jnp.float32)
    for outer in range(ITERS):
        pressure = relax(pressure, source, cond_pad, conductance, diagonal)
        surface = pressure[:, -1, ::stride].astype(jnp.bfloat16)
        copied = from_root(surface, "vol", last_vol)
        mine = lax.dynamic_slice_in_dim(copied, own_vol * half_count, half_count, 0)
        partial_rows = fold_traces(mine, plane)
        summed = lax.psum(partial_rows, "narrow")
        share = summed.shape[0] // lax.axis_size("narrow")
        traction = lax.dynamic_slice_in_dim(summed, lax.axis_index("narrow") * share, share, 0)
        if outer + 1 < ITERS:
            shared = lax.all_gather(traction, "vol", axis=1, tiled=True)
            placed = jnp.transpose(shared).reshape(excite, RY, RX)
            placed = jnp.pad(placed, ((0, 0), (0, cells_y - RY), (0, cells_x - RX)))
            source = forcing.at[:, -1].add(couple_gain * is_top * placed)
    return (pressure, traction)


def solution(mesh):
    placed = (
        P(None, "vol", "narrow", "wide"),
        P("vol", "narrow", "wide"),
        P(),
        P("wide", "narrow"),
    )
    return jax.shard_map(
        local,
        mesh=mesh,
        in_specs=placed,
        out_specs=(P(None, "vol", "narrow", "wide"), P(("wide", "narrow"), "vol")),
        check_vma=False,
    )
```

profile of v0, /device:TPU:64, one launch (start us, length us, event | category | flops | bytes accessed | tf_op | source)
XLA Modules:
  0.0 423.3 jit_solution(2321841271998520856)
XLA Ops:
  2.3 6.8 %broadcast_multiply_fusion.5 = (f32[2,192,128]{2,1,0:T(8,128)}, f32[2,192,128]{2,1,0:T(8,128)S(1)}) fusion(f32[]{:T(128)} %bitcast.7, s32[2,192,128]{2,1,0:T(8,128)} %param.7, f32[]{:T(128)} %bitcast.6, f32[]{:T(128)} %bitcast.5, f32[]{:T(128)} %bitcast.4, f32[]{:T(128)} %bitcast.3, f32[]{:T(128)} %bitcast.2, f32[]{:T(128)} %bitcast.1, f32[]{:T(128)} %bitcast), kind=kLoop, calls=%fused_computation.113 | loop fusion | flops 1179648 | bytes 589856 | tf_op jit(solution)/shard_map/mul | solution.py:56
  14.3 3.5 collective-permute-start.2
  17.7 8.1 %collective-permute-start.3 = (f32[4,192,1]{2,1,0:T(8,128)S(1)}, f32[4,192,1]{2,1,0:T(8,128)S(1)}, u32[]{:S(2)}, u32[]{:S(2)}) collective-permute-start(f32[4,192,1]{2,1,0:T(8,128)S(1)} %get-tuple-element.63), channel_id=1, source_target_pairs={{2,0},{4,2},{6,4},{8,6},{10,8},{12,10},{14,12},{16,14},{18,16},{20... | collective-permute-start | bytes 9224 | tf_op jit(solution)/shard_map/ppermute | solution.py:27
  25.8 7.2 %collective-permute-done.2 = f32[4,192,1]{2,1,0:T(8,128)S(1)} collective-permute-done((f32[4,192,1]{2,1,0:T(8,128)S(1)}, f32[4,192,1]{2,1,0:T(8,128)S(1)}, u32[]{:S(2)}, u32[]{:S(2)}) %collective-permute-start.2) | collective-permute-done | bytes 3104 | tf_op jit(solution)/shard_map/ppermute | solution.py:26
  34.3 3.5 collective-permute-start.4
  40.5 3.0 collective-permute-start.6
  47.7 9.6 %collective-permute-start.9 = (f32[2,4,192,1]{2,1,3,0:T(4,128)S(1)}, f32[2,4,192,1]{2,1,3,0:T(4,128)S(1)}, u32[]{:S(2)}, u32[]{:S(2)}) collective-permute-start(f32[2,4,192,1]{2,1,3,0:T(4,128)S(1)} %copy.20), channel_id=1, source_target_pairs={{2,0},{4,2},{6,4},{8,6},{10,8},{12,10},{14,12},{16,14},{18,16},{20... | collective-permute-start | bytes 18440 | tf_op jit(solution)/shard_map/ppermute | solution.py:27
  57.3 1.9 collective-permute-start.8
  60.0 8.5 %collective-permute-done.8 = f32[2,4,192,1]{2,1,3,0:T(4,128)S(1)} collective-permute-done((f32[2,4,192,1]{2,1,3,0:T(4,128)S(1)}, f32[2,4,192,1]{2,1,3,0:T(4,128)S(1)}, u32[]{:S(2)}, u32[]{:S(2)}) %collective-permute-start.8) | collective-permute-done | bytes 6176 | tf_op jit(solution)/shard_map/ppermute | solution.py:26
  69.3 5.1 %collective-permute-start.10 = (f32[2,4,1,130]{3,2,0,1:T(1,128)S(1)}, f32[2,4,1,130]{3,2,0,1:T(1,128)S(1)}, u32[]{:S(2)}, u32[]{:S(2)}) collective-permute-start(f32[2,4,1,130]{3,2,0,1:T(1,128)S(1)} %get-tuple-element.42), channel_id=1, source_target_pairs={{0,1},{2,3},{4,5},{6,7},{8,9},{10,11},{12,13},{14,15},{16,17},{18,... | collective-permute-start | bytes 12488 | tf_op jit(solution)/shard_map/ppermute | solution.py:26
  76.9 3.0 collective-permute-done.11
  87.3 2.0 collective-permute-done.13
  90.7 1.9 collective-permute-start.14
  93.0 9.6 %collective-permute-start.15 = (f32[2,4,192,1]{2,1,3,0:T(4,128)S(1)}, f32[2,4,192,1]{2,1,3,0:T(4,128)S(1)}, u32[]{:S(2)}, u32[]{:S(2)}) collective-permute-start(f32[2,4,192,1]{2,1,3,0:T(4,128)S(1)} %copy.25), channel_id=1, source_target_pairs={{2,0},{4,2},{6,4},{8,6},{10,8},{12,10},{14,12},{16,14},{18,16},{20... | collective-permute-start | bytes 18440 | tf_op jit(solution)/shard_map/ppermute | solution.py:27
  108.1 22.3 %copy.43 = bf16[128,65536]{0,1:T(8,128)(2,1)} copy(bf16[128,65536]{1,0:T(8,128)(2,1)} %param.9) | data formatting | bytes 33554432 | tf_op jit(solution)/shard_map/reshape | solution.py:98
  134.5 2.5 psum.28
  137.0 95.6 %all_gather.9 = bf16[1,16,4096]{2,1,0:T(8,128)(2,1)S(1)} all-gather(bf16[1,16,128]{2,1,0:T(8,128)(2,1)S(1)} %constant_dynamic-slice_fusion.3), channel_id=1, replica_groups=mesh['vol'=2,'wide'=32,'narrow'=2] {'wide'}, dimensions={2}, use_global_device_ids=true | all-gather | bytes 135168 | tf_op jit(solution)/shard_map/all_gather | solution.py:76
  235.5 8.3 %convolution_bitcast_fusion.1 = f32[128,1]{0,1:T(1,128)S(1)} fusion(bf16[128,16,4096]{0,2,1:T(8,128)(2,1)} %bitcast.31, bf16[16,4096,1]{1,0,2:T(8,128)(2,1)S(1)} %bitcast.33), kind=kOutput, calls=%fused_computation.5 | convolution fusion | flops 16777216 | bytes 16908800 | tf_op jit(solution)/shard_map/ryx,kyx->rk/dot_general | solution.py:73
  243.7 6.1 %psum.29 = f32[128,1]{0,1:T(1,128)S(1)} all-reduce(f32[128,1]{0,1:T(1,128)S(1)} %convolution_bitcast_fusion.1), channel_id=1, replica_groups=mesh['vol'=2,'wide'=32,'narrow'=2] {'narrow'}, use_global_device_ids=true, to_apply=%region_1.2 | all-reduce | flops 128 | bytes 1024 | tf_op jit(solution)/shard_map/psum | solution.py:109
  251.3 1.9 collective-permute-start.21
  253.2 3.9 collective-permute-start.20
  259.0 5.5 %collective-permute-done.20 = f32[2,4,192,1]{2,1,3,0:T(4,128)S(1)} collective-permute-done((f32[2,4,192,1]{2,1,3,0:T(4,128)S(1)}, f32[2,4,192,1]{2,1,3,0:T(4,128)S(1)}, u32[]{:S(2)}, u32[]{:S(2)}) %collective-permute-start.20) | collective-permute-done | bytes 6176 | tf_op jit(solution)/shard_map/ppermute | solution.py:26
  266.1 4.0 collective-permute-start.22
  271.4 4.2 collective-permute-done.23
  282.3 2.0 collective-permute-done.25
  285.6 1.9 collective-permute-start.26
  287.9 9.6 %collective-permute-start.27 = (f32[2,4,192,1]{2,1,3,0:T(4,128)S(1)}, f32[2,4,192,1]{2,1,3,0:T(4,128)S(1)}, u32[]{:S(2)}, u32[]{:S(2)}) collective-permute-start(f32[2,4,192,1]{2,1,3,0:T(4,128)S(1)} %copy.36), channel_id=1, source_target_pairs={{2,0},{4,2},{6,4},{8,6},{10,8},{12,10},{14,12},{16,14},{18,16},{20... | collective-permute-start | bytes 18440 | tf_op jit(solution)/shard_map/ppermute | solution.py:27
  303.1 4.2 collective-permute-done.29
  310.6 2.5 psum.30
  313.1 95.6 %all_gather.11 = bf16[1,16,4096]{2,1,0:T(8,128)(2,1)S(1)} all-gather(bf16[1,16,128]{2,1,0:T(8,128)(2,1)S(1)} %constant_dynamic-slice_fusion.1), channel_id=1, replica_groups=mesh['vol'=2,'wide'=32,'narrow'=2] {'wide'}, dimensions={2}, use_global_device_ids=true | all-gather | bytes 135168 | tf_op jit(solution)/shard_map/all_gather | solution.py:76
  408.7 8.3 %convolution_bitcast_fusion = f32[128,1]{0,1:T(1,128)S(1)} fusion(bf16[128,16,4096]{0,2,1:T(8,128)(2,1)} %bitcast.32, bf16[16,4096,1]{1,0,2:T(8,128)(2,1)S(1)} %bitcast.34), kind=kOutput, calls=%fused_computation.4 | convolution fusion | flops 16777216 | bytes 16908800 | tf_op jit(solution)/shard_map/ryx,kyx->rk/dot_general | solution.py:73
  417.0 4.9 %psum.31 = f32[128,1]{0,1:T(1,128)S(1)} all-reduce(f32[128,1]{0,1:T(1,128)S(1)} %convolution_bitcast_fusion), channel_id=1, replica_groups=mesh['vol'=2,'wide'=32,'narrow'=2] {'narrow'}, use_global_device_ids=true, to_apply=%region_3.4 | all-reduce | flops 128 | bytes 1024 | tf_op jit(solution)/shard_map/psum | solution.py:109
  (150 shorter events, 64.5 us)
Async XLA Ops:
  9.1 3.1 collective-permute-start
  10.8 3.2 collective-permute-start.1
  14.3 18.8 %collective-permute-start.2 = (f32[4,192,1]{2,1,0:T(8,128)S(1)}, f32[4,192,1]{2,1,0:T(8,128)S(1)}, u32[]{:S(2)}, u32[]{:S(2)}) collective-permute-start(f32[4,192,1]{2,1,0:T(8,128)S(1)} %get-tuple-element.62), channel_id=1, source_target_pairs={{0,2},{2,4},{4,6},{6,8},{8,10},{10,12},{12,14},{14,16},{16,18},{18... | collective-permute-start | bytes 9224 | tf_op jit(solution)/shard_map/ppermute | solution.py:26
  17.7 16.5 %collective-permute-start.3 = (f32[4,192,1]{2,1,0:T(8,128)S(1)}, f32[4,192,1]{2,1,0:T(8,128)S(1)}, u32[]{:S(2)}, u32[]{:S(2)}) collective-permute-start(f32[4,192,1]{2,1,0:T(8,128)S(1)} %get-tuple-element.63), channel_id=1, source_target_pairs={{2,0},{4,2},{6,4},{8,6},{10,8},{12,10},{14,12},{16,14},{18,16},{20... | collective-permute-start | bytes 9224 | tf_op jit(solution)/shard_map/ppermute | solution.py:27
  34.3 9.2 %collective-permute-start.4 = (f32[4,1,130]{2,1,0:T(1,128)S(1)}, f32[4,1,130]{2,1,0:T(1,128)S(1)}, u32[]{:S(2)}, u32[]{:S(2)}) collective-permute-start(f32[4,1,130]{2,1,0:T(1,128)S(1)} %get-tuple-element.44), channel_id=1, source_target_pairs={{0,1},{2,3},{4,5},{6,7},{8,9},{10,11},{12,13},{14,15},{16,17},{18,... | collective-permute-start | bytes 6248 | tf_op jit(solution)/shard_map/ppermute | solution.py:26
  37.9 5.7 %collective-permute-start.5 = (f32[4,1,130]{2,1,0:T(1,128)S(1)}, f32[4,1,130]{2,1,0:T(1,128)S(1)}, u32[]{:S(2)}, u32[]{:S(2)}) collective-permute-start(f32[4,1,130]{2,1,0:T(1,128)S(1)} %get-tuple-element.45), channel_id=1, source_target_pairs={{1,0},{3,2},{5,4},{7,6},{9,8},{11,10},{13,12},{15,14},{17,16},{19,... | collective-permute-start | bytes 6248 | tf_op jit(solution)/shard_map/ppermute | solution.py:27
  39.2 5.1 %collective-permute-start.7 = (f32[2,1,192,128]{3,2,0,1:T(8,128)S(1)}, f32[2,1,192,128]{3,2,0,1:T(8,128)S(1)}, u32[]{:S(2)}, u32[]{:S(2)}) collective-permute-start(f32[2,1,192,128]{3,2,0,1:T(8,128)S(1)} %broadcast.51), channel_id=1, source_target_pairs={{64,0},{65,1},{66,2},{67,3},{68,4},{69,5},{70,6},{71,7},{72,8},{73... | collective-permute-start | bytes 589832 | tf_op jit(solution)/shard_map/ppermute | solution.py:27
  40.5 4.1 collective-permute-start.6
  44.6 24.6 %copy-start.7 = (f32[2,1,192,128]{3,2,0,1:T(8,128)}, f32[2,1,192,128]{3,2,0,1:T(8,128)S(1)}, u32[]{:S(2)}) copy-start(f32[2,1,192,128]{3,2,0,1:T(8,128)S(1)} %collective-permute-done.6) | copy-start | bytes 589828
  47.7 21.2 %collective-permute-start.9 = (f32[2,4,192,1]{2,1,3,0:T(4,128)S(1)}, f32[2,4,192,1]{2,1,3,0:T(4,128)S(1)}, u32[]{:S(2)}, u32[]{:S(2)}) collective-permute-start(f32[2,4,192,1]{2,1,3,0:T(4,128)S(1)} %copy.20), channel_id=1, source_target_pairs={{2,0},{4,2},{6,4},{8,6},{10,8},{12,10},{14,12},{16,14},{18,16},{20... | collective-permute-start | bytes 18440 | tf_op jit(solution)/shard_map/ppermute | solution.py:27
  57.3 11.3 %collective-permute-start.8 = (f32[2,4,192,1]{2,1,3,0:T(4,128)S(1)}, f32[2,4,192,1]{2,1,3,0:T(4,128)S(1)}, u32[]{:S(2)}, u32[]{:S(2)}) collective-permute-start(f32[2,4,192,1]{2,1,3,0:T(4,128)S(1)} %copy.19), channel_id=1, source_target_pairs={{0,2},{2,4},{4,6},{6,8},{8,10},{10,12},{12,14},{14,16},{16,18},{18... | collective-permute-start | bytes 18440 | tf_op jit(solution)/shard_map/ppermute | solution.py:26
  69.3 7.6 %collective-permute-start.10 = (f32[2,4,1,130]{3,2,0,1:T(1,128)S(1)}, f32[2,4,1,130]{3,2,0,1:T(1,128)S(1)}, u32[]{:S(2)}, u32[]{:S(2)}) collective-permute-start(f32[2,4,1,130]{3,2,0,1:T(1,128)S(1)} %get-tuple-element.42), channel_id=1, source_target_pairs={{0,1},{2,3},{4,5},{6,7},{8,9},{10,11},{12,13},{14,15},{16,17},{18,... | collective-permute-start | bytes 12488 | tf_op jit(solution)/shard_map/ppermute | solution.py:26
  74.4 5.5 %collective-permute-start.11 = (f32[2,4,1,130]{3,2,0,1:T(1,128)S(1)}, f32[2,4,1,130]{3,2,0,1:T(1,128)S(1)}, u32[]{:S(2)}, u32[]{:S(2)}) collective-permute-start(f32[2,4,1,130]{3,2,0,1:T(1,128)S(1)} %get-tuple-element.43), channel_id=1, source_target_pairs={{1,0},{3,2},{5,4},{7,6},{9,8},{11,10},{13,12},{15,14},{17,16},{19,... | collective-permute-start | bytes 12488 | tf_op jit(solution)/shard_map/ppermute | solution.py:27
  76.9 56.4 %copy-start = (f32[2,192,128]{2,1,0:T(8,128)}, f32[2,192,128]{2,1,0:T(8,128)S(1)}, u32[]{:S(2)}) copy-start(f32[2,192,128]{2,1,0:T(8,128)S(1)} %get-tuple-element.31) | copy-start | bytes 589828
  84.7 2.6 collective-permute-start.12
  86.0 3.3 collective-permute-start.13
  90.7 11.9 %collective-permute-start.14 = (f32[2,4,192,1]{2,1,3,0:T(4,128)S(1)}, f32[2,4,192,1]{2,1,3,0:T(4,128)S(1)}, u32[]{:S(2)}, u32[]{:S(2)}) collective-permute-start(f32[2,4,192,1]{2,1,3,0:T(4,128)S(1)} %copy.24), channel_id=1, source_target_pairs={{0,2},{2,4},{4,6},{6,8},{8,10},{10,12},{12,14},{14,16},{16,18},{18... | collective-permute-start | bytes 18440 | tf_op jit(solution)/shard_map/ppermute | solution.py:26
  93.0 11.0 %collective-permute-start.15 = (f32[2,4,192,1]{2,1,3,0:T(4,128)S(1)}, f32[2,4,192,1]{2,1,3,0:T(4,128)S(1)}, u32[]{:S(2)}, u32[]{:S(2)}) collective-permute-start(f32[2,4,192,1]{2,1,3,0:T(4,128)S(1)} %copy.25), channel_id=1, source_target_pairs={{2,0},{4,2},{6,4},{8,6},{10,8},{12,10},{14,12},{16,14},{18,16},{20... | collective-permute-start | bytes 18440 | tf_op jit(solution)/shard_map/ppermute | solution.py:27
  105.1 25.3 %collective-permute-start.16 = (f32[2,4,1,130]{3,2,0,1:T(1,128)S(1)}, f32[2,4,1,130]{3,2,0,1:T(1,128)S(1)}, u32[]{:S(2)}, u32[]{:S(2)}) collective-permute-start(f32[2,4,1,130]{3,2,0,1:T(1,128)S(1)} %get-tuple-element.40), channel_id=1, source_target_pairs={{0,1},{2,3},{4,5},{6,7},{8,9},{10,11},{12,13},{14,15},{16,17},{18,... | collective-permute-start | bytes 12488 | tf_op jit(solution)/shard_map/ppermute | solution.py:26
  106.8 23.6 %collective-permute-start.17 = (f32[2,4,1,130]{3,2,0,1:T(1,128)S(1)}, f32[2,4,1,130]{3,2,0,1:T(1,128)S(1)}, u32[]{:S(2)}, u32[]{:S(2)}) collective-permute-start(f32[2,4,1,130]{3,2,0,1:T(1,128)S(1)} %get-tuple-element.41), channel_id=1, source_target_pairs={{1,0},{3,2},{5,4},{7,6},{9,8},{11,10},{13,12},{15,14},{17,16},{19,... | collective-permute-start | bytes 12488 | tf_op jit(solution)/shard_map/ppermute | solution.py:27
  232.7 17.2 %collective-permute-start.18 = (f32[2,1,192,128]{3,2,0,1:T(8,128)S(1)}, f32[2,1,192,128]{3,2,0,1:T(8,128)S(1)}, u32[]{:S(2)}, u32[]{:S(2)}) collective-permute-start(f32[2,1,192,128]{3,2,0,1:T(8,128)S(1)} %get-tuple-element.56), channel_id=1, source_target_pairs={{0,64},{1,65},{2,66},{3,67},{4,68},{5,69},{6,70},{7,71},{8,72},{9,... | collective-permute-start | bytes 589832 | tf_op jit(solution)/shard_map/ppermute | solution.py:26
  234.0 15.9 %collective-permute-start.19 = (f32[2,1,192,128]{3,2,0,1:T(8,128)S(1)}, f32[2,1,192,128]{3,2,0,1:T(8,128)S(1)}, u32[]{:S(2)}, u32[]{:S(2)}) collective-permute-start(f32[2,1,192,128]{3,2,0,1:T(8,128)S(1)} %get-tuple-element.57), channel_id=1, source_target_pairs={{64,0},{65,1},{66,2},{67,3},{68,4},{69,5},{70,6},{71,7},{72,8},{73... | collective-permute-start | bytes 589832 | tf_op jit(solution)/shard_map/ppermute | solution.py:27
  251.3 13.5 %collective-permute-start.21 = (f32[2,4,192,1]{2,1,3,0:T(4,128)S(1)}, f32[2,4,192,1]{2,1,3,0:T(4,128)S(1)}, u32[]{:S(2)}, u32[]{:S(2)}) collective-permute-start(f32[2,4,192,1]{2,1,3,0:T(4,128)S(1)} %copy.32), channel_id=1, source_target_pairs={{2,0},{4,2},{6,4},{8,6},{10,8},{12,10},{14,12},{16,14},{18,16},{20... | collective-permute-start | bytes 18440 | tf_op jit(solution)/shard_map/ppermute | solution.py:27
  253.2 11.3 %collective-permute-start.20 = (f32[2,4,192,1]{2,1,3,0:T(4,128)S(1)}, f32[2,4,192,1]{2,1,3,0:T(4,128)S(1)}, u32[]{:S(2)}, u32[]{:S(2)}) collective-permute-start(f32[2,4,192,1]{2,1,3,0:T(4,128)S(1)} %copy.31), channel_id=1, source_target_pairs={{0,2},{2,4},{4,6},{6,8},{8,10},{10,12},{12,14},{14,16},{16,18},{18... | collective-permute-start | bytes 18440 | tf_op jit(solution)/shard_map/ppermute | solution.py:26
  266.1 5.3 %collective-permute-start.22 = (f32[2,4,1,130]{3,2,0,1:T(1,128)S(1)}, f32[2,4,1,130]{3,2,0,1:T(1,128)S(1)}, u32[]{:S(2)}, u32[]{:S(2)}) collective-permute-start(f32[2,4,1,130]{3,2,0,1:T(1,128)S(1)} %get-tuple-element.38), channel_id=1, source_target_pairs={{0,1},{2,3},{4,5},{6,7},{8,9},{10,11},{12,13},{14,15},{16,17},{18,... | collective-permute-start | bytes 12488 | tf_op jit(solution)/shard_map/ppermute | solution.py:26
  270.1 5.5 %collective-permute-start.23 = (f32[2,4,1,130]{3,2,0,1:T(1,128)S(1)}, f32[2,4,1,130]{3,2,0,1:T(1,128)S(1)}, u32[]{:S(2)}, u32[]{:S(2)}) collective-permute-start(f32[2,4,1,130]{3,2,0,1:T(1,128)S(1)} %get-tuple-element.39), channel_id=1, source_target_pairs={{1,0},{3,2},{5,4},{7,6},{9,8},{11,10},{13,12},{15,14},{17,16},{19,... | collective-permute-start | bytes 12488 | tf_op jit(solution)/shard_map/ppermute | solution.py:27
  279.6 2.6 collective-permute-start.24
  280.9 3.3 collective-permute-start.25
  285.6 11.9 %collective-permute-start.26 = (f32[2,4,192,1]{2,1,3,0:T(4,128)S(1)}, f32[2,4,192,1]{2,1,3,0:T(4,128)S(1)}, u32[]{:S(2)}, u32[]{:S(2)}) collective-permute-start(f32[2,4,192,1]{2,1,3,0:T(4,128)S(1)} %copy.35), channel_id=1, source_target_pairs={{0,2},{2,4},{4,6},{6,8},{8,10},{10,12},{12,14},{14,16},{16,18},{18... | collective-permute-start | bytes 18440 | tf_op jit(solution)/shard_map/ppermute | solution.py:26
  287.9 11.0 %collective-permute-start.27 = (f32[2,4,192,1]{2,1,3,0:T(4,128)S(1)}, f32[2,4,192,1]{2,1,3,0:T(4,128)S(1)}, u32[]{:S(2)}, u32[]{:S(2)}) collective-permute-start(f32[2,4,192,1]{2,1,3,0:T(4,128)S(1)} %copy.36), channel_id=1, source_target_pairs={{2,0},{4,2},{6,4},{8,6},{10,8},{12,10},{14,12},{16,14},{18,16},{20... | collective-permute-start | bytes 18440 | tf_op jit(solution)/shard_map/ppermute | solution.py:27
  300.1 3.0 collective-permute-start.28
  301.8 5.5 %collective-permute-start.29 = (f32[2,4,1,130]{3,2,0,1:T(1,128)S(1)}, f32[2,4,1,130]{3,2,0,1:T(1,128)S(1)}, u32[]{:S(2)}, u32[]{:S(2)}) collective-permute-start(f32[2,4,1,130]{3,2,0,1:T(1,128)S(1)} %get-tuple-element.37), channel_id=1, source_target_pairs={{1,0},{3,2},{5,4},{7,6},{9,8},{11,10},{13,12},{15,14},{17,16},{19,... | collective-permute-start | bytes 12488 | tf_op jit(solution)/shard_map/ppermute | solution.py:27
  (16 other events, 50.4 us)
where the time goes:
time: 425 us; the launch traced here: 423 us
  blocking collectives  209 us (49%)
  starting transfers between devices  89.7 us (21%)
  waiting for transfers between devices  42.2 us (10%)
  local copies, waits for them, and re-layouts  39.4 us (9%)
  other arithmetic  24.9 us (6%)
  matrix products  16.5 us (4%)
    all_gather x2, blocking collectives, fold_traces(): lax.all_gather(mine, 'wide', axis=2, tiled=True)  191 us
    ppermute x15, starting transfers between devices, with_halo(): after = lax.ppermute(first, axis, down)  52 us
    ppermute x15, starting transfers between devices, with_halo(): before = lax.ppermute(last, axis, up)  37.8 us
    reshape x1, local copies, waits for them, and re-layouts, local(): plane = boundary_operator.reshape(tile_rows, BY, -1)  22.3 us
    ppermute x15, waiting for transfers between devices, with_halo(): before = lax.ppermute(last, axis, up)  21.6 us
    ppermute x15, waiting for transfers between devices, with_halo(): after = lax.ppermute(first, axis, down)  20.6 us
    dot_general x2, matrix products, fold_traces(): jnp.einsum('ryx,kyx->rk', plane, lax.all_gather(mine, 'wide', axis=2, til...  16.5 us
    mul x5, other arithmetic, apply_operator(): weighted = box_sum(padded * cond_pad) - conductance * center  11.6 us
  transfers between devices with their start and end apart: 30, of which 13 were waited for; matrix products, arithmetic and copies ran while one was open for 8% of the time, Pallas kernels for 0%

commit v1 on v0

v1 whole, which is shorter than its diff:
```python
import functools

import jax
import jax.numpy as jnp
from jax import lax
from jax.experimental import pallas as pl
from jax.experimental.pallas import tpu as pltpu
from jax.sharding import PartitionSpec as P

MESH = pl.DeviceIdType.MESH

BY = 16
RX = 64
MAT = 8

lower_edge = 0.25
upper_edge = 1.75
couple_gain = 40.0

middle = (upper_edge + lower_edge) / 2.0
spread = (upper_edge - lower_edge) / 2.0
center_ratio = middle / spread
ratio_0 = 1.0 / center_ratio
ratio_1 = 1.0 / (2.0 * center_ratio - ratio_0)
gain0 = 1.0 / middle
keep1 = ratio_1 * ratio_0
gain1 = 2.0 * ratio_1 / spread

CY = 192
CX = 128
NZ = 4
PAD = 16
ROWS_ALL = PAD + CY + PAD
HALO = 8
CHUNK = 16
CHUNKS = (CY + 2 * HALO) // CHUNK
SLOT = 8
GROUPS = 4
GROUP_ROWS = CY // GROUPS


def select_materials(ids, materials):
    value = jnp.full(ids.shape, materials[0], jnp.float32)
    for number in range(1, MAT):
        value = jnp.where(ids == number, materials[number], value)
    return value


def kernel(
    wide_count,
    forcing,
    ids,
    materials,
    op,
    out_p,
    out_t,
    fv,
    iv,
    f,
    c,
    inv,
    m,
    pa,
    qa,
    pb,
    qb,
    strip,
    corner,
    got_strip,
    got_corner,
    opv,
    g1,
    g2,
    g3,
    part,
    got_part,
    last_part,
    got_last,
    local_sem,
    op_sem,
    s_send,
    s_recv,
    g_send,
    g_recv,
    x_send,
    x_recv,
    o_send,
    o_recv,
    o_local,
):
    v = lax.axis_index("vol")
    w = lax.axis_index("wide")
    n = lax.axis_index("narrow")
    other_v = 1 - v
    other_n = 1 - n
    right = lax.rem(w + 1, wide_count)
    left = lax.rem(w + wide_count - 1, wide_count)

    def device(vol, wide, narrow):
        return {"vol": vol, "wide": wide, "narrow": narrow}

    barrier = pltpu.get_barrier_semaphore()

    def greet(vol, wide, narrow):
        pl.semaphore_signal(
            barrier, inc=1, device_id=device(vol, wide, narrow), device_id_type=MESH
        )

    greet(other_v, w, n)
    for k in (0, 1):
        greet(k, w, other_n)
        for side in (left, right):
            greet(k, side, other_n)
    for side in (left, right):
        greet(other_v, side, n)

    def greet_wide(j, carry):
        greet(v, lax.rem(w + j, wide_count), n)
        return carry

    lax.fori_loop(1, wide_count, greet_wide, 0)

    load_ids = pltpu.make_async_copy(ids, iv, local_sem.at[0])
    load_f = pltpu.make_async_copy(forcing, fv, local_sem.at[1])
    load_own = pltpu.make_async_copy(
        forcing.at[v], f.at[0, pl.ds(2 * v, 2), pl.ds(PAD, CY), :], local_sem.at[2]
    )
    load_ids.start()
    load_f.start()
    load_own.start()

    zeros8 = jnp.zeros((8, CX), jnp.float32)
    for ref in (c, pa, qa, pb, qb):
        for t in (0, 1):
            for z in range(NZ):
                ref[t, z, 0:8, :] = zeros8
                ref[t, z, ROWS_ALL - 8 : ROWS_ALL, :] = zeros8
    outside = pl.multiple_of(PAD - HALO + other_n * 0 + n * (CY + HALO), 8)
    inside = pl.multiple_of(PAD - HALO + other_n * (CY + HALO), 8)
    for ref in (f, c):
        for t in (0, 1):
            for z in range(NZ):
                ref[t, z, pl.ds(outside, 8), :] = zeros8

    load_ids.wait()
    for layer in (0, 1):
        c[0, 2 * v + layer, PAD : PAD + CY, :] = select_materials(iv[layer], materials)
    load_f.wait()

    span = wide_count * CX

    def op_chunk(s):
        columns = pl.ds(pl.multiple_of(s * span, span), span)
        return pltpu.make_async_copy(op.at[:, columns], opv.at[:, columns], op_sem.at[s])

    edge_row = pl.multiple_of(other_n * (CY - 8), 8)
    lane = lax.broadcasted_iota(jnp.int32, (GROUP_ROWS, CX), 1)
    lane8 = lax.broadcasted_iota(jnp.int32, (8, CX), 1)
    for k in (0, 1):
        packed = jnp.zeros((GROUP_ROWS, CX), jnp.float32)
        edge = jnp.zeros((8, CX), jnp.float32)
        for field in range(4):
            for group in range(GROUPS):
                rows = pl.ds(group * GROUP_ROWS, GROUP_ROWS)
                if field < 2:
                    x = fv[k, field, rows, :]
                else:
                    x = c[0, 2 * v + field - 2, pl.ds(PAD + group * GROUP_ROWS, GROUP_ROWS), :]
                at = group * 4 * SLOT + field * SLOT
                x = pltpu.roll(x, (at + 4) % CX, 1)
                packed = jnp.where((lane >= at) & (lane < at + SLOT), x, packed)
            if field < 2:
                x = fv[k, field, pl.ds(edge_row, 8), :]
            else:
                x = c[0, 2 * v + field - 2, pl.ds(PAD + edge_row, 8), :]
            at = field * SLOT
            x = pltpu.roll(x, at + 4, 1)
            edge = jnp.where((lane8 >= at) & (lane8 < at + SLOT), x, edge)
        strip[k] = packed
        corner[k] = edge

    pl.semaphore_wait(barrier, wide_count - 1 + 9)

    sends = []

    def send(src, dst, send_sem, recv_sem, where):
        copy = pltpu.make_async_remote_copy(
            src_ref=src,
            dst_ref=dst,
            send_sem=send_sem,
            recv_sem=recv_sem,
            device_id=where,
            device_id_type=MESH,
        )
        copy.start()
        sends.append(copy)
        return copy

    own_layers = pl.ds(2 * v, 2)
    there_row = pl.multiple_of(PAD - HALO + n * (CY + HALO), 8)
    for k in (0, 1):
        for direction, side in ((0, right), (1, left)):
            send(
                strip.at[k],
                got_strip.at[direction, v],
                s_send.at[6 + 2 * direction + k],
                s_recv.at[6 + 2 * direction + v],
                device(k, side, n),
            )
    send(
        fv.at[other_v],
        f.at[0, own_layers, pl.ds(PAD, CY), :],
        s_send.at[0],
        s_recv.at[0],
        device(other_v, w, n),
    )
    own_block = c.at[0, own_layers, pl.ds(PAD, CY), :]
    send(own_block, own_block, s_send.at[1], s_recv.at[1], device(other_v, w, n))
    for k in (0, 1):
        send(
            fv.at[k, :, pl.ds(edge_row, 8), :],
            f.at[0, own_layers, pl.ds(there_row, 8), :],
            s_send.at[2 + k],
            s_recv.at[2 + v],
            device(k, w, other_n),
        )
        send(
            c.at[0, own_layers, pl.ds(pl.multiple_of(PAD + edge_row, 8), 8), :],
            c.at[0, own_layers, pl.ds(there_row, 8), :],
            s_send.at[4 + k],
            s_recv.at[4 + v],
            device(k, w, other_n),
        )
        for direction, side in ((0, right), (1, left)):
            send(
                corner.at[k],
                got_corner.at[direction, v],
                s_send.at[10 + 2 * direction + k],
                s_recv.at[10 + 2 * direction + v],
                device(k, side, other_n),
            )

    def start_op(s, carry):
        op_chunk(s).start()
        return carry

    lax.fori_loop(0, BY, start_op, 0)

    def wait_bytes(ref, sem):
        pltpu.make_async_copy(ref, ref, sem).wait()

    has_left = w > 0
    has_right = w < wide_count - 1
    for direction in (0, 1):
        for vol in (0, 1):
            wait_bytes(got_strip.at[direction, vol], s_recv.at[6 + 2 * direction + vol])
            wait_bytes(got_corner.at[direction, vol], s_recv.at[10 + 2 * direction + vol])
    keep_left = jnp.where(has_left, 1.0, 0.0)
    keep_right = jnp.where(has_right, 1.0, 0.0)
    for z in range(NZ):
        vol = z // 2
        from_left = lax.rem(lane, SLOT) < 4
        merged = jnp.where(
            from_left, got_strip[0, vol] * keep_left, got_strip[1, vol] * keep_right
        )
        from_left8 = lax.rem(lane8, SLOT) < 4
        merged8 = jnp.where(
            from_left8, got_corner[0, vol] * keep_left, got_corner[1, vol] * keep_right
        )
        for which, ref in ((0, f), (2, c)):
            field = which + z % 2
            for group in range(GROUPS):
                at = group * 4 * SLOT + field * SLOT
                x = pltpu.roll(merged, (CX - 4 - at) % CX, 1)
                x = jnp.where((lane < 4) | (lane >= CX - 4), x, 0.0)
                ref[1, z, pl.ds(PAD + group * GROUP_ROWS, GROUP_ROWS), :] = x
            at = field * SLOT
            x = pltpu.roll(merged8, (CX - 4 - at) % CX, 1)
            x = jnp.where((lane8 < 4) | (lane8 >= CX - 4), x, 0.0)
            ref[1, z, pl.ds(inside, 8), :] = x
    load_own.wait()
    wait_bytes(f.at[0, pl.ds(2 * other_v, 2), pl.ds(PAD, CY), :], s_recv.at[0])
    wait_bytes(c.at[0, pl.ds(2 * other_v, 2), pl.ds(PAD, CY), :], s_recv.at[1])
    for vol in (0, 1):
        wait_bytes(f.at[0, pl.ds(2 * vol, 2), pl.ds(inside, 8), :], s_recv.at[2 + vol])
        wait_bytes(c.at[0, pl.ds(2 * vol, 2), pl.ds(inside, 8), :], s_recv.at[4 + vol])

    lane_c = lax.broadcasted_iota(jnp.int32, (CHUNK, CX), 1)
    first = lane_c == 0
    final = lane_c == CX - 1

    def box(ref, r, tiles=2):
        ys = [
            [
                ref[t, z, pl.ds(r - 1, CHUNK), :]
                + ref[t, z, pl.ds(r, CHUNK), :]
                + ref[t, z, pl.ds(r + 1, CHUNK), :]
                for z in range(NZ)
            ]
            for t in (0, 1)
        ]
        sums = []
        for y in ys:
            low, high = y[0] + y[1], y[2] + y[3]
            sums.append((low, low + y[2], y[1] + high, high))
        result = [[], []]
        for z in range(NZ):
            center, side = sums[0][z], sums[1][z]
            center_up, side_up = pltpu.roll(center, 1, 1), pltpu.roll(side, 1, 1)
            center_down, side_down = (
                pltpu.roll(center, CX - 1, 1),
                pltpu.roll(side, CX - 1, 1),
            )
            result[0].append(
                center
                + jnp.where(first, side_up, center_up)
                + jnp.where(final, side_down, center_down)
            )
            if tiles == 2:
                result[1].append(
                    side
                    + jnp.where(first, center_up, side_up)
                    + jnp.where(final, center_down, side_down)
                )
        return result

    def rows_of(i):
        return pl.multiple_of(PAD - HALO + i * CHUNK, 8)

    def first_sweep(i, carry):
        r = rows_of(i)
        sums = box(c, r)
        for t in (0, 1):
            for z in range(NZ):
                cond = c[t, z, pl.ds(r, CHUNK), :]
                diagonal = 38.5 * cond + 0.5 * sums[t][z]
                inverse = jnp.where(cond > 0.0, 1.0 / diagonal, 0.0)
                inv[t, z, pl.ds(r, CHUNK), :] = inverse
                u = gain0 * f[t, z, pl.ds(r, CHUNK), :] * inverse
                pa[t, z, pl.ds(r, CHUNK), :] = u
                qa[t, z, pl.ds(r, CHUNK), :] = cond * u
        return carry

    def sweep(p, q, r, use, tiles=2):
        p_sums, q_sums = box(p, r, tiles), box(q, r, tiles)
        for t in range(tiles):
            for z in range(NZ):
                at = (t, z, pl.ds(r, CHUNK), slice(None))
                cond = c[at]
                u = p[at]
                scaled = (
                    f[at] + 0.5 * (cond * p_sums[t][z] + q_sums[t][z]) - q[at]
                ) * inv[at] - u
                use(at, cond, u, scaled)

    def second_sweep(i, carry):
        def use(at, cond, u, scaled):
            u = (1.0 + keep1) * u + gain1 * scaled
            pb[at] = u
            qb[at] = cond * u

        sweep(pa, qa, rows_of(i), use)
        return carry

    def third_sweep(i, carry):
        def use(at, cond, u, scaled):
            moved = gain0 * scaled
            u = u + moved
            m[at] = moved
            pa[at] = u
            qa[at] = cond * u

        sweep(pb, qb, rows_of(i), use)
        return carry

    def fourth_sweep(i, carry):
        def use(at, cond, u, scaled):
            pb[at] = u + (keep1 * m[at] + gain1 * scaled)

        sweep(pa, qa, rows_of(i), use, 1)
        return carry

    my_columns = pl.ds(pl.multiple_of(w * CX, CX), CX)

    def share(g, number):
        def to(j, carry):
            pltpu.make_async_remote_copy(
                src_ref=g.at[:, my_columns],
                dst_ref=g.at[:, my_columns],
                send_sem=g_send.at[number],
                recv_sem=g_recv.at[number],
                device_id=device(v, lax.rem(w + j, wide_count), n),
                device_id_type=MESH,
            ).start()
            return carry

        lax.fori_loop(1, wide_count, to, 0)

    def trace():
        return pb[0, NZ - 1, pl.ds(PAD, BY, stride=CY // BY), :].astype(jnp.bfloat16)

    row16 = lax.broadcasted_iota(jnp.int32, (BY, CX), 0)

    def product(g, low, high, fetch=False):
        def add(s, total):
            if fetch:
                op_chunk(s).wait()
            block = opv[:, pl.ds(pl.multiple_of(s * span, span), span)]
            rows = lax.dot_general(
                g[...], block, (((1,), (1,)), ((), ())), preferred_element_type=jnp.float32
            )
            return total + jnp.where(row16 == s, rows, 0.0)

        total = lax.fori_loop(low, high, add, jnp.zeros((BY, CX), jnp.float32))
        return jnp.sum(total, axis=0, keepdims=True)

    lax.fori_loop(0, CHUNKS, first_sweep, 0)
    lax.fori_loop(0, CHUNKS, second_sweep, 0)
    g1[:, my_columns] = trace()
    share(g1, 0)
    lax.fori_loop(0, CHUNKS, third_sweep, 0)
    lax.fori_loop(0, CHUNKS, fourth_sweep, 0)
    g2[:, my_columns] = trace()
    share(g2, 1)

    def store_rows(number, y, count):
        here = out_p.at[v, :, pl.ds(y, count), :]
        own = pltpu.make_async_copy(
            pb.at[0, own_layers, pl.ds(PAD + y, count), :], here, o_local.at[number]
        )
        own.start()
        send(
            pb.at[0, pl.ds(2 * other_v, 2), pl.ds(PAD + y, count), :],
            here,
            o_send.at[number],
            o_recv.at[number],
            device(other_v, w, n),
        )
        return own

    stores = [store_rows(0, 8, CY - 16)]

    wait_bytes(g1.at[:, CX:], g_recv.at[0])
    part1 = product(g1, 0, BY, True)
    part[...] = jnp.broadcast_to(part1, (8, CX))
    for number, (side, narrow) in enumerate(((w, other_n), (left, n), (left, other_n))):
        send(
            part,
            got_part.at[number],
            x_send.at[number],
            x_recv.at[number],
            device(v, side, narrow),
        )
    wait_bytes(g2.at[:, CX:], g_recv.at[1])
    part2 = product(g2, 1, BY)
    for number in range(3):
        wait_bytes(got_part.at[number], x_recv.at[number])

    here = part[...] + got_part[0]
    beyond = got_part[1] + got_part[2]
    here_high, beyond_high = pltpu.roll(here, CX - RX, 1), pltpu.roll(beyond, CX - RX, 1)
    is_first = n == 0
    row8 = lax.broadcasted_iota(jnp.int32, (8, CX), 0)

    def source_row(low, high, width, flag):
        return jnp.where(lane8 < width, couple_gain * jnp.where(flag, low, high), 0.0)[0:1]

    delta_own = source_row(here, here_high, RX, is_first)
    delta_side = source_row(beyond, beyond_high, 1, is_first)
    below = jnp.where(is_first, 1.0, 0.0)
    delta_below = below * source_row(here_high, here_high, RX, is_first)
    delta_below_side = below * source_row(beyond_high, beyond_high, 1, is_first)
    lane1 = lax.broadcasted_iota(jnp.int32, (1, CX), 1)

    def x_sum(center, side):
        return (
            center
            + pltpu.roll(jnp.broadcast_to(center, (8, CX)), 1, 1)[0:1]
            + jnp.where(
                lane1 == CX - 1,
                pltpu.roll(jnp.broadcast_to(side, (8, CX)), CX - 1, 1)[0:1],
                pltpu.roll(jnp.broadcast_to(center, (8, CX)), CX - 1, 1)[0:1],
            )
        )

    def added(delta, side, row, tile_row, near, at_target):
        q_center = gain0 * delta * inv[0, NZ - 1, row : row + 1, :]
        q_side = gain0 * side * inv[1, NZ - 1, row : row + 1, :]
        s_q = jnp.where(near, x_sum(q_center, q_side), 0.0)
        s_cq = jnp.where(
            near,
            x_sum(
                c[0, NZ - 1, row : row + 1, :] * q_center,
                c[1, NZ - 1, row : row + 1, :] * q_side,
            ),
            0.0,
        )
        for z in (NZ - 2, NZ - 1):
            rows = pl.ds(tile_row, 8)
            cond = c[0, z, rows, :]
            inverse = inv[0, z, rows, :]
            change = gain1 * 0.5 * (cond * s_q + s_cq) * inverse
            if z == NZ - 1 and at_target is not None:
                q = jnp.where(at_target, q_center, 0.0)
                source = jnp.where(at_target, delta, 0.0)
                change = (
                    change
                    + (1.0 + keep1) * q
                    + gain1 * ((source - cond * q) * inverse - q)
                )
            pb[0, z, rows, :] = pb[0, z, rows, :] + change

    added(delta_own, delta_side, PAD, PAD, row8 <= 1, row8 == 0)
    added(delta_below, delta_below_side, PAD + CY, PAD + CY - 8, row8 == 7, None)
    g3[:, my_columns] = trace()
    share(g3, 2)
    stores.append(store_rows(1, 0, 8))
    stores.append(store_rows(2, CY - 8, 8))

    wait_bytes(g3.at[:, CX:], g_recv.at[2])
    last = part2 + product(g3, 0, 1)
    last_part[...] = jnp.broadcast_to(last, (8, CX))
    send(last_part, got_last, x_send.at[3], x_recv.at[3], device(v, w, other_n))
    wait_bytes(got_last, x_recv.at[3])
    traction = last_part[...] + got_last[...]
    traction = jnp.where(is_first, traction, pltpu.roll(traction, CX - RX, 1))
    turned = jnp.transpose(jnp.broadcast_to(traction[0:1], (CX, CX)))
    out_t[...] = turned[0:RX, 0:1]

    for own in stores:
        own.wait()
    for number, (y, count) in enumerate(((8, CY - 16), (0, 8), (CY - 8, 8))):
        wait_bytes(out_p.at[other_v, :, pl.ds(y, count), :], o_recv.at[number])
    for copy in sends:
        copy.wait_send()
    for number, g in enumerate((g1, g2, g3)):
        wait_bytes(g.at[:, CX:], g_send.at[number])


def local(forcing, material_ids, materials, boundary_operator):
    wide_count = lax.axis_size("wide")
    field = pltpu.VMEM((2, NZ, ROWS_ALL, CX), jnp.float32)
    gathered = pltpu.VMEM((BY, wide_count * CX), jnp.bfloat16)
    dma = pltpu.SemaphoreType.DMA
    anywhere = pl.BlockSpec(memory_space=pl.ANY)
    rows = boundary_operator.shape[0]
    return pl.pallas_call(
        functools.partial(kernel, wide_count),
        out_shape=(
            jax.ShapeDtypeStruct(forcing.shape, jnp.float32),
            jax.ShapeDtypeStruct((RX, 1), jnp.float32),
        ),
        in_specs=[
            anywhere,
            anywhere,
            pl.BlockSpec(memory_space=pltpu.SMEM),
            anywhere,
        ],
        out_specs=(anywhere, pl.BlockSpec(memory_space=pltpu.VMEM)),
        scratch_shapes=[
            pltpu.VMEM(forcing.shape, jnp.float32),
            pltpu.VMEM(material_ids.shape, jnp.int32),
            field,
            field,
            field,
            field,
            field,
            field,
            field,
            field,
            pltpu.VMEM((2, GROUP_ROWS, CX), jnp.float32),
            pltpu.VMEM((2, 8, CX), jnp.float32),
            pltpu.VMEM((2, 2, GROUP_ROWS, CX), jnp.float32),
            pltpu.VMEM((2, 2, 8, CX), jnp.float32),
            pltpu.VMEM(boundary_operator.shape, jnp.bfloat16),
            gathered,
            gathered,
            gathered,
            pltpu.VMEM((8, CX), jnp.float32),
            pltpu.VMEM((3, 8, CX), jnp.float32),
            pltpu.VMEM((8, CX), jnp.float32),
            pltpu.VMEM((8, CX), jnp.float32),
            dma((3,)),
            dma((BY,)),
            dma((14,)),
            dma((14,)),
            dma((3,)),
            dma((3,)),
            dma((4,)),
            dma((4,)),
            dma((3,)),
            dma((3,)),
            dma((3,)),
        ],
        compiler_params=pltpu.CompilerParams(
            collective_id=0, has_side_effects=True, vmem_limit_bytes=48 * 1024 * 1024
        ),
        cost_estimate=pl.CostEstimate(
            flops=4 * rows * boundary_operator.shape[1],
            bytes_accessed=2 * rows * boundary_operator.shape[1],
            transcendentals=0,
        ),
    )(forcing, material_ids, materials, boundary_operator)


def solution(mesh):
    placed = (
        P(None, "vol", "narrow", "wide"),
        P("vol", "narrow", "wide"),
        P(),
        P("wide", "narrow"),
    )
    return jax.shard_map(
        local,
        mesh=mesh,
        in_specs=placed,
        out_specs=(P(None, "vol", "narrow", "wide"), P(("wide", "narrow"), "vol")),
        check_vma=False,
    )
```

time: 425 us -> 51.5 us (0.12)
  the two profiles are of different devices: /device:TPU:64 before, /device:TPU:1 now
where the time goes in v1:
time: 51.5 us; the launch traced here: 50.5 us
  Pallas kernels  46 us (89%)
  local copies, waits for them, and re-layouts  3.9 us (8%)
  between operations  0.65 us (1%)
    pallas_call x1, Pallas kernels, local(): pl.pallas_call(functools.partial(kernel, wide_count), out_shape=(jax.Shap...  46 us
    unnamed x7, local copies, waits for them, and re-layouts  3.32 us

profile of v1, /device:TPU:1, one launch (start us, length us, event | category | flops | bytes accessed | tf_op | source)
XLA Modules:
  0.0 50.5 jit_solution(17829837316058595718)
XLA Ops:
  0.6 0.0 copy-start
  0.6 1.0 %copy-done = f32[2,2,192,128]{3,2,1,0:T(8,128)S(1)} copy-done((f32[2,2,192,128]{3,2,1,0:T(8,128)S(1)}, f32[2,2,192,128]{3,2,1,0:T(8,128)}, u32[]{:S(2)}) %copy-start) | copy-done | bytes 393240
  1.6 0.0 copy-start.1
  1.6 0.9 %copy-done.1 = s32[2,192,128]{2,1,0:T(8,128)S(1)} copy-done((s32[2,192,128]{2,1,0:T(8,128)S(1)}, s32[2,192,128]{2,1,0:T(8,128)}, u32[]{:S(2)}) %copy-start.1) | copy-done | bytes 196632
  2.6 0.0 copy-start.2
  2.6 0.7 %copy-done.2 = f32[8]{0:T(128)S(1)} copy-done((f32[8]{0:T(128)S(1)}, f32[8]{0:T(128)}, u32[]{:S(2)}) %copy-start.2) | copy-done | bytes 56
  3.2 46.0 %shard_map.59 = (f32[2,2,192,128]{3,2,1,0:T(8,128)S(1)}, f32[64,1]{1,0:T(8,128)S(1)}) custom-call(f32[2,2,192,128]{3,2,1,0:T(8,128)S(1)} %copy-done, s32[2,192,128]{2,1,0:T(8,128)S(1)} %copy-done.1, f32[8]{0:T(128)S(1)} %copy-done.2, bf16[128,65536]{1,0:T(8,128)(2,1)} %op.1), custom_call_target="tpu_custom_call" | custom-call | flops 33554432 | bytes 16777216 | tf_op jit(solution)/shard_map/pallas_call | solution.py:547
  49.2 0.6 %copy.6 = f32[64,1]{0,1:T(1,128)} copy(f32[64,1]{1,0:T(8,128)S(1)} %get-tuple-element.3) | data formatting | bytes 512 | tf_op jit(solution)/shard_map/pallas_call | solution.py:547
  49.8 0.7 %copy.8 = f32[2,2,192,128]{3,2,1,0:T(8,128)} copy(f32[2,2,192,128]{3,2,1,0:T(8,128)S(1)} %get-tuple-element.6) | data formatting | bytes 786432
Async XLA Ops:
  0.6 1.0 %copy-start = (f32[2,2,192,128]{3,2,1,0:T(8,128)S(1)}, f32[2,2,192,128]{3,2,1,0:T(8,128)}, u32[]{:S(2)}) copy-start(f32[2,2,192,128]{3,2,1,0:T(8,128)} %forcing.1) | copy-start | bytes 1179652
  1.6 0.9 %copy-start.1 = (s32[2,192,128]{2,1,0:T(8,128)S(1)}, s32[2,192,128]{2,1,0:T(8,128)}, u32[]{:S(2)}) copy-start(s32[2,192,128]{2,1,0:T(8,128)} %ids.1) | copy-start | bytes 589828
  2.6 0.7 %copy-start.2 = (f32[8]{0:T(128)S(1)}, f32[8]{0:T(128)}, u32[]{:S(2)}) copy-start(f32[8]{0:T(128)} %materials.1) | copy-start | bytes 100

commit v2 on v1

--- a/solution.py
+++ b/solution.py
@@ -37,6 +37,7 @@
 SLOT = 8
 GROUPS = 4
 GROUP_ROWS = CY // GROUPS
+QUAD = 4
 
 
 def select_materials(ids, materials):
@@ -69,13 +70,15 @@
     got_strip,
     got_corner,
     opv,
+    own_trace,
     g1,
     g2,
-    g3,
     part,
-    got_part,
-    last_part,
-    got_last,
+    total,
+    coef,
+    part2_own,
+    part2_got,
+    op_other,
     local_sem,
     op_sem,
     s_send,
@@ -87,6 +90,7 @@
     o_send,
     o_recv,
     o_local,
+    q_recv,
 ):
     v = lax.axis_index("vol")
     w = lax.axis_index("wide")
@@ -106,16 +110,14 @@
             barrier, inc=1, device_id=device(vol, wide, narrow), device_id_type=MESH
         )
 
-    greet(other_v, w, n)
-    for k in (0, 1):
-        greet(k, w, other_n)
-        for side in (left, right):
-            greet(k, side, other_n)
-    for side in (left, right):
-        greet(other_v, side, n)
+    for narrow in (n, other_n):
+        for side in (left, w, right):
+            greet(other_v, side, narrow)
+    greet(v, w, other_n)
 
     def greet_wide(j, carry):
-        greet(v, lax.rem(w + j, wide_count), n)
+        for narrow in (n, other_n):
+            greet(v, lax.rem(w + j, wide_count), narrow)
         return carry
 
     lax.fori_loop(1, wide_count, greet_wide, 0)
@@ -179,7 +181,7 @@
         strip[k] = packed
         corner[k] = edge
 
-    pl.semaphore_wait(barrier, wide_count - 1 + 9)
+    pl.semaphore_wait(barrier, 2 * wide_count - 1 + 6)
 
     sends = []
 
@@ -289,35 +291,39 @@
     first = lane_c == 0
     final = lane_c == CX - 1
 
-    def box(ref, r, tiles=2):
-        ys = [
-            [
-                ref[t, z, pl.ds(r - 1, CHUNK), :]
+    def box(ref, r, layers, tiles):
+        inner = range(max(layers[0] - 1, 0), min(layers[-1] + 2, NZ))
+        sums = []
+        for t in (0, 1):
+            y = {
+                z: ref[t, z, pl.ds(r - 1, CHUNK), :]
                 + ref[t, z, pl.ds(r, CHUNK), :]
                 + ref[t, z, pl.ds(r + 1, CHUNK), :]
-                for z in range(NZ)
-            ]
-            for t in (0, 1)
-        ]
-        sums = []
-        for y in ys:
-            low, high = y[0] + y[1], y[2] + y[3]
-            sums.append((low, low + y[2], y[1] + high, high))
-        result = [[], []]
-        for z in range(NZ):
+                for z in inner
+            }
+            low = y[0] + y[1] if 0 in layers or 1 in layers else None
+            high = y[2] + y[3] if 2 in layers or 3 in layers else None
+            made = {}
+            for z in layers:
+                made[z] = (
+                    low if z == 0 else high if z == 3 else low + y[2] if z == 1 else y[1] + high
+                )
+            sums.append(made)
+        result = ({}, {})
+        for z in layers:
             center, side = sums[0][z], sums[1][z]
             center_up, side_up = pltpu.roll(center, 1, 1), pltpu.roll(side, 1, 1)
             center_down, side_down = (
                 pltpu.roll(center, CX - 1, 1),
                 pltpu.roll(side, CX - 1, 1),
             )
-            result[0].append(
+            result[0][z] = (
                 center
                 + jnp.where(first, side_up, center_up)
                 + jnp.where(final, side_down, center_down)
             )
-            if tiles == 2:
-                result[1].append(
+            if 1 in tiles:
+                result[1][z] = (
                     side
                     + jnp.where(first, center_up, side_up)
                     + jnp.where(final, center_down, side_down)
@@ -327,24 +333,27 @@
     def rows_of(i):
         return pl.multiple_of(PAD - HALO + i * CHUNK, 8)
 
-    def first_sweep(i, carry):
+    both = (0, 1)
+
+    def first_sweep(i, layers):
         r = rows_of(i)
-        sums = box(c, r)
-        for t in (0, 1):
-            for z in range(NZ):
-                cond = c[t, z, pl.ds(r, CHUNK), :]
+        sums = box(c, r, layers, both)
+        for t in both:
+            for z in layers:
+                at = (t, z, pl.ds(r, CHUNK), slice(None))
+                cond = c[at]
                 diagonal = 38.5 * cond + 0.5 * sums[t][z]
                 inverse = jnp.where(cond > 0.0, 1.0 / diagonal, 0.0)
-                inv[t, z, pl.ds(r, CHUNK), :] = inverse
-                u = gain0 * f[t, z, pl.ds(r, CHUNK), :] * inverse
-                pa[t, z, pl.ds(r, CHUNK), :] = u
-                qa[t, z, pl.ds(r, CHUNK), :] = cond * u
-        return carry
-
-    def sweep(p, q, r, use, tiles=2):
-        p_sums, q_sums = box(p, r, tiles), box(q, r, tiles)
-        for t in range(tiles):
-            for z in range(NZ):
+                inv[at] = inverse
+                u = gain0 * f[at] * inverse
+                pa[at] = u
+                qa[at] = cond * u
+
+    def sweep(p, q, i, use, layers, tiles):
+        r = rows_of(i)
+        p_sums, q_sums = box(p, r, layers, tiles), box(q, r, layers, tiles)
+        for t in tiles:
+            for z in layers:
                 at = (t, z, pl.ds(r, CHUNK), slice(None))
                 cond = c[at]
                 u = p[at]
@@ -353,16 +362,15 @@
                 ) * inv[at] - u
                 use(at, cond, u, scaled)
 
-    def second_sweep(i, carry):
+    def second_sweep(i, layers, tiles):
         def use(at, cond, u, scaled):
             u = (1.0 + keep1) * u + gain1 * scaled
             pb[at] = u
             qb[at] = cond * u
 
-        sweep(pa, qa, rows_of(i), use)
-        return carry
-
-    def third_sweep(i, carry):
+        sweep(pa, qa, i, use, layers, tiles)
+
+    def third_sweep(i, layers):
         def use(at, cond, u, scaled):
             moved = gain0 * scaled
             u = u + moved
@@ -370,58 +378,185 @@
             pa[at] = u
             qa[at] = cond * u
 
-        sweep(pb, qb, rows_of(i), use)
-        return carry
-
-    def fourth_sweep(i, carry):
+        sweep(pb, qb, i, use, layers, both)
+
+    def fourth_sweep(i, layers):
         def use(at, cond, u, scaled):
             pb[at] = u + (keep1 * m[at] + gain1 * scaled)
 
-        sweep(pa, qa, rows_of(i), use, 1)
-        return carry
+        sweep(pa, qa, i, use, layers, (0,))
+
+    def for_chunks(step):
+        def body(i, carry):
+            step(i)
+            return carry
+
+        lax.fori_loop(0, CHUNKS, body, 0, unroll=CHUNKS)
 
     my_columns = pl.ds(pl.multiple_of(w * CX, CX), CX)
 
-    def share(g, number):
+    def share(block, numbers, narrows):
         def to(j, carry):
+            for number, narrow in zip(numbers, narrows):
+                pltpu.make_async_remote_copy(
+                    src_ref=block,
+                    dst_ref=block,
+                    send_sem=g_send.at[number],
+                    recv_sem=g_recv.at[number],
+                    device_id=device(v, lax.rem(w + j, wide_count), narrow),
+                    device_id_type=MESH,
+                ).start()
+            return carry
+
+        lax.fori_loop(1, wide_count, to, 0)
+        if len(numbers) == 2:
             pltpu.make_async_remote_copy(
-                src_ref=g.at[:, my_columns],
-                dst_ref=g.at[:, my_columns],
-                send_sem=g_send.at[number],
-                recv_sem=g_recv.at[number],
-                device_id=device(v, lax.rem(w + j, wide_count), n),
+                src_ref=block,
+                dst_ref=block,
+                send_sem=g_send.at[numbers[1]],
+                recv_sem=g_recv.at[numbers[1]],
+                device_id=device(v, w, other_n),
                 device_id_type=MESH,
             ).start()
-            return carry
-
-        lax.fori_loop(1, wide_count, to, 0)
 
     def trace():
         return pb[0, NZ - 1, pl.ds(PAD, BY, stride=CY // BY), :].astype(jnp.bfloat16)
 
     row16 = lax.broadcasted_iota(jnp.int32, (BY, CX), 0)
 
-    def product(g, low, high, fetch=False):
+    def product(g, low, high):
         def add(s, total):
-            if fetch:
-                op_chunk(s).wait()
             block = opv[:, pl.ds(pl.multiple_of(s * span, span), span)]
             rows = lax.dot_general(
                 g[...], block, (((1,), (1,)), ((), ())), preferred_element_type=jnp.float32
             )
             return total + jnp.where(row16 == s, rows, 0.0)
 
-        total = lax.fori_loop(low, high, add, jnp.zeros((BY, CX), jnp.float32))
+        total = lax.fori_loop(
+            low, high, add, jnp.zeros((BY, CX), jnp.float32), unroll=5
+        )
         return jnp.sum(total, axis=0, keepdims=True)
 
-    lax.fori_loop(0, CHUNKS, first_sweep, 0)
-    lax.fori_loop(0, CHUNKS, second_sweep, 0)
-    g1[:, my_columns] = trace()
-    share(g1, 0)
-    lax.fori_loop(0, CHUNKS, third_sweep, 0)
-    lax.fori_loop(0, CHUNKS, fourth_sweep, 0)
+    quads = wide_count // QUAD
+    my_quad, my_place = w // QUAD, lax.rem(w, QUAD)
+
+    def quad_at(d, sign):
+        if quads % QUAD:
+            return lax.rem(my_quad + sign * d + quads, quads)
+        high, low = my_quad // QUAD, lax.rem(my_quad, QUAD)
+        rings = quads // QUAD
+        high = lax.rem(high + sign * (d // QUAD) + rings, rings)
+        low = lax.rem(low + sign * lax.rem(d, QUAD) + QUAD, QUAD)
+        return high * QUAD + low
+
+    def share_first():
+        def to(i, carry):
+            d = i // QUAD
+            place = lax.rem(my_place + lax.rem(i, QUAD), QUAD)
+            pltpu.make_async_remote_copy(
+                src_ref=own_trace,
+                dst_ref=g1.at[:, my_columns],
+                send_sem=g_send.at[0],
+                recv_sem=q_recv.at[d],
+                device_id=device(v, quad_at(d, 1) * QUAD + place, n),
+                device_id_type=MESH,
+            ).start()
+            return carry
+
+        lax.fori_loop(1, wide_count, lambda i, carry: to(wide_count - i, carry), 0)
+        pltpu.make_async_copy(own_trace, g1.at[:, my_columns], q_recv.at[0]).start()
+
+    lanes = QUAD * CX
+
+    def product_first():
+        for s in range(BY):
+            op_chunk(s).wait()
+
+        def add(i, total):
+            step = lax.rem(i, QUAD)
+            d = i - step + step + step // 2 - 2 * (step // 3)
+            if quads % QUAD:
+                d = i
+            wait_bytes(g1.at[:, 0:lanes], q_recv.at[d])
+            first_lane = quad_at(d, -1) * lanes
+            x = g1[:, pl.ds(pl.multiple_of(first_lane, lanes), lanes)]
+            for s in range(BY):
+                block = opv[:, pl.ds(pl.multiple_of(s * span + first_lane, lanes), lanes)]
+                rows = lax.dot_general(
+                    x, block, (((1,), (1,)), ((), ())), preferred_element_type=jnp.float32
+                )
+                total = total + jnp.where(row16 == s, rows, 0.0)
+            return total
+
+        total = lax.fori_loop(0, quads, add, jnp.zeros((BY, CX), jnp.float32))
+        return jnp.sum(total, axis=0, keepdims=True)
+
+    for_chunks(lambda i: first_sweep(i, (2, 3)))
+    for_chunks(lambda i: second_sweep(i, (3,), (0,)))
+    own_trace[...] = trace()
+    share_first()
+
+    half = span // 2
+    my_half = pl.ds(pl.multiple_of(v * half, half), half)
+    their_half = pl.ds(pl.multiple_of(other_v * half, half), half)
+    send(
+        op.at[pl.ds(pl.multiple_of(other_n * RX, RX), RX), my_half],
+        op_other.at[:, my_half],
+        x_send.at[0],
+        x_recv.at[0],
+        device(v, w, other_n),
+    )
+
+    for_chunks(lambda i: first_sweep(i, (0, 1)))
+    for_chunks(lambda i: second_sweep(i, (1, 2, 3), both))
+    for_chunks(lambda i: third_sweep(i, (2, 3)))
+    for_chunks(lambda i: fourth_sweep(i, (3,)))
     g2[:, my_columns] = trace()
-    share(g2, 1)
+    share(g2.at[:, my_columns], (1,), (n,))
+
+    top = NZ - 1
+    lane1 = lax.broadcasted_iota(jnp.int32, (8, CX), 1)
+
+    def tile(ref, t, z, row):
+        return ref[t, z, row : row + 8, :]
+
+    def neighbours(ref, z, row):
+        center, side = tile(ref, 0, z, row), tile(ref, 1, z, row)
+        before = jnp.where(lane1 == 0, pltpu.roll(side, 1, 1), pltpu.roll(center, 1, 1))
+        after = jnp.where(
+            lane1 == CX - 1, pltpu.roll(side, CX - 1, 1), pltpu.roll(center, CX - 1, 1)
+        )
+        return before, after
+
+    cond8, inverse8 = tile(c, 0, top, PAD), tile(inv, 0, top, PAD)
+    cond_before, cond_after = neighbours(c, top, PAD)
+    inverse_before, inverse_after = neighbours(inv, top, PAD)
+    here8 = couple_gain * ((1.0 + keep1 - gain1) * gain0 + gain1) * inverse8
+    beside = 0.5 * couple_gain * gain1 * gain0 * inverse8
+    before8 = beside * (cond8 + cond_before) * inverse_before
+    after8 = beside * (cond8 + cond_after) * inverse_after
+    coef[n, 0:4, my_columns] = jnp.concatenate(
+        [tile(pb, 0, top, PAD)[0:1], here8[0:1], before8[0:1], after8[0:1]], axis=0
+    )
+    share(coef.at[n, 0:4, my_columns], (2, 3), (n, other_n))
+
+    part[n, 0:1, my_columns] = product_first()
+    share(part.at[n, 0:1, my_columns], (4, 5), (n, other_n))
+
+    wait_bytes(op_other.at[:, my_half], x_recv.at[0])
+    send(
+        op_other.at[:, my_half],
+        op_other.at[:, my_half],
+        x_send.at[1],
+        x_recv.at[1],
+        device(other_v, w, n),
+    )
+    wait_bytes(g2.at[:, CX:], g_recv.at[1])
+    part2_own[...] = jnp.broadcast_to(product(g2, 1, BY), (8, CX))
+    send(part2_own, part2_got, x_send.at[2], x_recv.at[2], device(v, w, other_n))
+    for_chunks(lambda i: second_sweep(i, (0,), both))
+    for_chunks(lambda i: third_sweep(i, (0, 1)))
+    for_chunks(lambda i: fourth_sweep(i, (0, 1, 2)))
 
     def store_rows(number, y, count):
         here = out_p.at[v, :, pl.ds(y, count), :]
@@ -440,67 +575,60 @@
 
     stores = [store_rows(0, 8, CY - 16)]
 
-    wait_bytes(g1.at[:, CX:], g_recv.at[0])
-    part1 = product(g1, 0, BY, True)
-    part[...] = jnp.broadcast_to(part1, (8, CX))
-    for number, (side, narrow) in enumerate(((w, other_n), (left, n), (left, other_n))):
-        send(
-            part,
-            got_part.at[number],
-            x_send.at[number],
-            x_recv.at[number],
-            device(v, side, narrow),
-        )
-    wait_bytes(g2.at[:, CX:], g_recv.at[1])
-    part2 = product(g2, 1, BY)
-    for number in range(3):
-        wait_bytes(got_part.at[number], x_recv.at[number])
-
-    here = part[...] + got_part[0]
-    beyond = got_part[1] + got_part[2]
+    wait_bytes(coef.at[0, 0:4, CX:], g_recv.at[2])
+    wait_bytes(coef.at[0, 0:4, :], g_recv.at[3])
+    wait_bytes(op_other.at[:, their_half], x_recv.at[1])
+    wait_bytes(part2_got, x_recv.at[2])
+    part2 = part2_own[...] + part2_got[...]
+    is_first = n == 0
+    part2 = jnp.where(is_first, part2, pltpu.roll(part2, CX - RX, 1))
+    part2_turned = jnp.transpose(jnp.broadcast_to(part2[0:1], (CX, CX)))[0:RX, 0:1]
+
+    wait_bytes(part.at[0, 0:1, CX:], g_recv.at[4])
+    wait_bytes(part.at[0, 0:1, :], g_recv.at[5])
+    total[0:1, :] = part[0, 0:1, :] + part[1, 0:1, :]
+
+    row8 = lax.broadcasted_iota(jnp.int32, (8, CX), 0)
+    here = jnp.broadcast_to(total[0:1, my_columns], (8, CX))
+    beyond = jnp.broadcast_to(
+        total[0:1, pl.ds(pl.multiple_of(right * CX, CX), CX)], (8, CX)
+    )
     here_high, beyond_high = pltpu.roll(here, CX - RX, 1), pltpu.roll(beyond, CX - RX, 1)
-    is_first = n == 0
-    row8 = lax.broadcasted_iota(jnp.int32, (8, CX), 0)
-
-    def source_row(low, high, width, flag):
-        return jnp.where(lane8 < width, couple_gain * jnp.where(flag, low, high), 0.0)[0:1]
-
-    delta_own = source_row(here, here_high, RX, is_first)
-    delta_side = source_row(beyond, beyond_high, 1, is_first)
+
+    def source_rows(low, high, width):
+        return jnp.where(lane8 < width, couple_gain * jnp.where(is_first, low, high), 0.0)
+
+    delta_own = source_rows(here, here_high, RX)
+    delta_side = source_rows(beyond, beyond_high, 1)
     below = jnp.where(is_first, 1.0, 0.0)
-    delta_below = below * source_row(here_high, here_high, RX, is_first)
-    delta_below_side = below * source_row(beyond_high, beyond_high, 1, is_first)
-    lane1 = lax.broadcasted_iota(jnp.int32, (1, CX), 1)
+    delta_below = below * source_rows(here_high, here_high, RX)
+    delta_below_side = below * source_rows(beyond_high, beyond_high, 1)
 
     def x_sum(center, side):
         return (
             center
-            + pltpu.roll(jnp.broadcast_to(center, (8, CX)), 1, 1)[0:1]
+            + pltpu.roll(center, 1, 1)
             + jnp.where(
-                lane1 == CX - 1,
-                pltpu.roll(jnp.broadcast_to(side, (8, CX)), CX - 1, 1)[0:1],
-                pltpu.roll(jnp.broadcast_to(center, (8, CX)), CX - 1, 1)[0:1],
+                lane8 == CX - 1, pltpu.roll(side, CX - 1, 1), pltpu.roll(center, CX - 1, 1)
             )
         )
 
     def added(delta, side, row, tile_row, near, at_target):
-        q_center = gain0 * delta * inv[0, NZ - 1, row : row + 1, :]
-        q_side = gain0 * side * inv[1, NZ - 1, row : row + 1, :]
+        def spread_row(ref, t):
+            return jnp.broadcast_to(ref[t, top, row : row + 1, :], (8, CX))
+
+        q_center = gain0 * delta * spread_row(inv, 0)
+        q_side = gain0 * side * spread_row(inv, 1)
         s_q = jnp.where(near, x_sum(q_center, q_side), 0.0)
         s_cq = jnp.where(
-            near,
-            x_sum(
-                c[0, NZ - 1, row : row + 1, :] * q_center,
-                c[1, NZ - 1, row : row + 1, :] * q_side,
-            ),
-            0.0,
-        )
-        for z in (NZ - 2, NZ - 1):
+            near, x_sum(spread_row(c, 0) * q_center, spread_row(c, 1) * q_side), 0.0
+        )
+        for z in (top - 1, top):
             rows = pl.ds(tile_row, 8)
             cond = c[0, z, rows, :]
             inverse = inv[0, z, rows, :]
             change = gain1 * 0.5 * (cond * s_q + s_cq) * inverse
-            if z == NZ - 1 and at_target is not None:
+            if z == top and at_target is not None:
                 q = jnp.where(at_target, q_center, 0.0)
                 source = jnp.where(at_target, delta, 0.0)
                 change = (
@@ -512,20 +640,36 @@
 
     added(delta_own, delta_side, PAD, PAD, row8 <= 1, row8 == 0)
     added(delta_below, delta_below_side, PAD + CY, PAD + CY - 8, row8 == 7, None)
-    g3[:, my_columns] = trace()
-    share(g3, 2)
     stores.append(store_rows(1, 0, 8))
     stores.append(store_rows(2, CY - 8, 8))
 
-    wait_bytes(g3.at[:, CX:], g_recv.at[2])
-    last = part2 + product(g3, 0, 1)
-    last_part[...] = jnp.broadcast_to(last, (8, CX))
-    send(last_part, got_last, x_send.at[3], x_recv.at[3], device(v, w, other_n))
-    wait_bytes(got_last, x_recv.at[3])
-    traction = last_part[...] + got_last[...]
-    traction = jnp.where(is_first, traction, pltpu.roll(traction, CX - RX, 1))
-    turned = jnp.transpose(jnp.broadcast_to(traction[0:1], (CX, CX)))
-    out_t[...] = turned[0:RX, 0:1]
+    lane_all = lax.broadcasted_iota(jnp.int32, (1, span), 1)
+    at_targets = lax.rem(lane_all, CX) < RX
+    traction = total[0:1, :]
+    rows = []
+    for half_n in (0, 1):
+        value = traction if half_n == 0 else pltpu.roll(traction, span - RX, 1)
+        value = jnp.where(at_targets, value, 0.0)
+        rows.append(
+            coef[half_n, 0:1, :]
+            + coef[half_n, 1:2, :] * value
+            + coef[half_n, 2:3, :] * pltpu.roll(value, 1, 1)
+            + coef[half_n, 3:4, :] * pltpu.roll(value, span - 1, 1)
+        )
+    own_row = jnp.where(is_first, rows[0], rows[1]).astype(jnp.bfloat16)
+    other_row = jnp.where(is_first, rows[1], rows[0]).astype(jnp.bfloat16)
+
+    def against(block, row):
+        return lax.dot_general(
+            block,
+            jnp.broadcast_to(row, (BY, span)),
+            (((1,), (1,)), ((), ())),
+            preferred_element_type=jnp.float32,
+        )
+
+    mine = opv[pl.ds(pl.multiple_of(n * RX, RX), RX), 0:span]
+    last = against(mine, own_row) + against(op_other[...], other_row)
+    out_t[...] = part2_turned + last[:, 0:1]
 
     for own in stores:
         own.wait()
@@ -533,8 +677,11 @@
         wait_bytes(out_p.at[other_v, :, pl.ds(y, count), :], o_recv.at[number])
     for copy in sends:
         copy.wait_send()
-    for number, g in enumerate((g1, g2, g3)):
+    for number, g in enumerate((g1, g2)):
         wait_bytes(g.at[:, CX:], g_send.at[number])
+    for number, ref, count in ((2, coef, 4), (4, part, 1)):
+        wait_bytes(ref.at[0, 0:count, CX:], g_send.at[number])
+        wait_bytes(ref.at[0, 0:count, :], g_send.at[number + 1])
 
 
 def local(forcing, material_ids, materials, boundary_operator):
@@ -543,7 +690,9 @@
     gathered = pltpu.VMEM((BY, wide_count * CX), jnp.bfloat16)
     dma = pltpu.SemaphoreType.DMA
     anywhere = pl.BlockSpec(memory_space=pl.ANY)
+    hbm = pl.BlockSpec(memory_space=pltpu.HBM)
     rows = boundary_operator.shape[0]
+    quads = wide_count // QUAD
     return pl.pallas_call(
         functools.partial(kernel, wide_count),
         out_shape=(
@@ -551,10 +700,10 @@
             jax.ShapeDtypeStruct((RX, 1), jnp.float32),
         ),
         in_specs=[
-            anywhere,
-            anywhere,
+            hbm,
+            hbm,
             pl.BlockSpec(memory_space=pltpu.SMEM),
-            anywhere,
+            hbm,
         ],
         out_specs=(anywhere, pl.BlockSpec(memory_space=pltpu.VMEM)),
         scratch_shapes=[
@@ -573,27 +722,30 @@
             pltpu.VMEM((2, 2, GROUP_ROWS, CX), jnp.float32),
             pltpu.VMEM((2, 2, 8, CX), jnp.float32),
             pltpu.VMEM(boundary_operator.shape, jnp.bfloat16),
+            pltpu.VMEM((BY, CX), jnp.bfloat16),
             gathered,
             gathered,
-            gathered,
-            pltpu.VMEM((8, CX), jnp.float32),
-            pltpu.VMEM((3, 8, CX), jnp.float32),
+            pltpu.VMEM((2, 8, wide_count * CX), jnp.float32),
+            pltpu.VMEM((8, wide_count * CX), jnp.float32),
+            pltpu.VMEM((2, 8, wide_count * CX), jnp.float32),
             pltpu.VMEM((8, CX), jnp.float32),
             pltpu.VMEM((8, CX), jnp.float32),
+            pltpu.VMEM((RX, wide_count * CX), jnp.bfloat16),
             dma((3,)),
             dma((BY,)),
             dma((14,)),
             dma((14,)),
-            dma((3,)),
-            dma((3,)),
-            dma((4,)),
-            dma((4,)),
+            dma((6,)),
+            dma((6,)),
             dma((3,)),
             dma((3,)),
             dma((3,)),
+            dma((3,)),
+            dma((3,)),
+            dma((quads,)),
         ],
         compiler_params=pltpu.CompilerParams(
-            collective_id=0, has_side_effects=True, vmem_limit_bytes=48 * 1024 * 1024
+            collective_id=0, has_side_effects=True, vmem_limit_bytes=62 * 1024 * 1024
         ),
         cost_estimate=pl.CostEstimate(
             flops=4 * rows * boundary_operator.shape[1],

time: 51.5 us -> 43.5 us (0.84); the launches traced: 50.5 us -> 43.2 us
  Pallas kernels: 46 us -> 39.5 us
  local copies, waits for them, and re-layouts: 3.9 us -> 3.11 us
    pallas_call x1, Pallas kernels: 46 us -> 39.5 us  [local(): pl.pallas_call(functools.partial(kernel, wide_count), out_shape=(jax.Shap...]
    unnamed x7 -> x1, local copies, waits for them, and re-layouts: 3.32 us -> 1.77 us
    pallas_call x1, local copies, waits for them, and re-layouts: 0.59 us -> 1.34 us  [local(): pl.pallas_call(functools.partial(kernel, wide_count), out_shape=(jax.Shap...]
where the time goes in v2:
time: 43.5 us; the launch traced here: 43.2 us
  Pallas kernels  39.5 us (91%)
  local copies, waits for them, and re-layouts  3.11 us (7%)
  between operations  0.64 us (1%)
    pallas_call x1, Pallas kernels, local(): pl.pallas_call(functools.partial(kernel, wide_count), out_shape=(jax.Shap...  39.5 us
    unnamed x1, local copies, waits for them, and re-layouts  1.77 us
    pallas_call x1, local copies, waits for them, and re-layouts, local(): pl.pallas_call(functools.partial(kernel, wide_count), out_shape=(jax.Shap...  1.34 us

profile of v2, /device:TPU:1, one launch (start us, length us, event | category | flops | bytes accessed | tf_op | source)
XLA Modules:
  0.0 43.2 jit_solution(55701857320105930)
XLA Ops:
  0.6 39.5 %shard_map.59 = (f32[2,2,192,128]{3,2,1,0:T(8,128)}, f32[64,1]{1,0:T(8,128)}) custom-call(f32[2,2,192,128]{3,2,1,0:T(8,128)} %forcing.1, s32[2,192,128]{2,1,0:T(8,128)} %ids.1, f32[8]{0:T(128)} %materials.1, bf16[128,65536]{1,0:T(8,128)(2,1)} %op.1), custom_call_target="tpu_custom_call" | custom-call | flops 33554432 | bytes 16777216 | tf_op jit(solution)/shard_map/pallas_call | solution.py:696
  40.1 1.3 %copy.6 = f32[64,1]{0,1:T(1,128)} copy(f32[64,1]{1,0:T(8,128)} %get-tuple-element.3) | data formatting | bytes 512 | tf_op jit(solution)/shard_map/pallas_call | solution.py:696
  41.4 1.8 %copy.8 = f32[2,2,192,128]{3,2,1,0:T(8,128)} copy(f32[2,2,192,128]{3,2,1,0:T(8,128)} %get-tuple-element.6) | data formatting | bytes 786432

commit v3 on v2

--- a/solution.py
+++ b/solution.py
@@ -78,6 +78,7 @@
     coef,
     part2_own,
     part2_got,
+    row_t,
     op_other,
     local_sem,
     op_sem,
@@ -91,6 +92,7 @@
     o_recv,
     o_local,
     q_recv,
+    relay,
 ):
     v = lax.axis_index("vol")
     w = lax.axis_index("wide")
@@ -105,22 +107,53 @@
 
     barrier = pltpu.get_barrier_semaphore()
 
+    def signal(semaphore, vol, wide, narrow):
+        pl.semaphore_signal(
+            semaphore, inc=1, device_id=device(vol, wide, narrow), device_id_type=MESH
+        )
+
+    greeted = []
+
     def greet(vol, wide, narrow):
-        pl.semaphore_signal(
-            barrier, inc=1, device_id=device(vol, wide, narrow), device_id_type=MESH
-        )
+        signal(barrier, vol, wide, narrow)
+        greeted.append(0)
 
     for narrow in (n, other_n):
         for side in (left, w, right):
             greet(other_v, side, narrow)
+        for side in (left, right):
+            greet(v, side, narrow)
     greet(v, w, other_n)
 
-    def greet_wide(j, carry):
-        for narrow in (n, other_n):
-            greet(v, lax.rem(w + j, wide_count), narrow)
-        return carry
-
-    lax.fori_loop(1, wide_count, greet_wide, 0)
+    quads = wide_count // QUAD
+    my_quad, my_place = w // QUAD, lax.rem(w, QUAD)
+    staged = quads == 2 * QUAD
+
+    def quad_at(d, sign):
+        if not staged:
+            return lax.rem(my_quad + sign * d + quads, quads)
+        high, low = my_quad // QUAD, lax.rem(my_quad, QUAD)
+        high = lax.rem(high + d // QUAD, 2)
+        low = lax.rem(low + sign * lax.rem(d, QUAD) + QUAD, QUAD)
+        return high * QUAD + low
+
+    y_ring = [my_quad * QUAD + lax.rem(my_place + j, QUAD) for j in range(1, QUAD)]
+    if staged:
+        for j in range(1, QUAD):
+            greet(v, y_ring[j - 1], n)
+            greet(v, quad_at(j, 1) * QUAD + my_place, n)
+        opposite = lax.rem(w + wide_count // 2, wide_count)
+        greet(v, opposite, n)
+        greet(v, opposite, other_n)
+    else:
+
+        def greet_wide(j, carry):
+            for narrow in (n, other_n):
+                signal(barrier, v, lax.rem(w + j, wide_count), narrow)
+            return carry
+
+        lax.fori_loop(1, wide_count, greet_wide, 0)
+        greeted.extend([0] * (2 * (wide_count - 1)))
 
     load_ids = pltpu.make_async_copy(ids, iv, local_sem.at[0])
     load_f = pltpu.make_async_copy(forcing, fv, local_sem.at[1])
@@ -181,7 +214,10 @@
         strip[k] = packed
         corner[k] = edge
 
-    pl.semaphore_wait(barrier, 2 * wide_count - 1 + 6)
+    pl.semaphore_wait(barrier, len(greeted))
+    if staged:
+        for place in y_ring:
+            signal(relay.at[0], v, place, n)
 
     sends = []
 
@@ -247,6 +283,10 @@
         return carry
 
     lax.fori_loop(0, BY, start_op, 0)
+    if staged:
+        pl.semaphore_wait(relay.at[0], QUAD - 1)
+        for wide, narrow in ((opposite, n), (opposite, other_n), (w, other_n)):
+            signal(relay.at[1], v, wide, narrow)
 
     def wait_bytes(ref, sem):
         pltpu.make_async_copy(ref, ref, sem).wait()
@@ -396,7 +436,8 @@
     my_columns = pl.ds(pl.multiple_of(w * CX, CX), CX)
 
     def share(block, numbers, narrows):
-        def to(j, carry):
+        def to(i, carry):
+            j = 1 + lax.rem(i + wide_count // 2 - 1, wide_count - 1)
             for number, narrow in zip(numbers, narrows):
                 pltpu.make_async_remote_copy(
                     src_ref=block,
@@ -408,7 +449,7 @@
                 ).start()
             return carry
 
-        lax.fori_loop(1, wide_count, to, 0)
+        lax.fori_loop(0, wide_count - 1, to, 0)
         if len(numbers) == 2:
             pltpu.make_async_remote_copy(
                 src_ref=block,
@@ -436,18 +477,6 @@
             low, high, add, jnp.zeros((BY, CX), jnp.float32), unroll=5
         )
         return jnp.sum(total, axis=0, keepdims=True)
-
-    quads = wide_count // QUAD
-    my_quad, my_place = w // QUAD, lax.rem(w, QUAD)
-
-    def quad_at(d, sign):
-        if quads % QUAD:
-            return lax.rem(my_quad + sign * d + quads, quads)
-        high, low = my_quad // QUAD, lax.rem(my_quad, QUAD)
-        rings = quads // QUAD
-        high = lax.rem(high + sign * (d // QUAD) + rings, rings)
-        low = lax.rem(low + sign * lax.rem(d, QUAD) + QUAD, QUAD)
-        return high * QUAD + low
 
     def share_first():
         def to(i, carry):
@@ -475,7 +504,7 @@
         def add(i, total):
             step = lax.rem(i, QUAD)
             d = i - step + step + step // 2 - 2 * (step // 3)
-            if quads % QUAD:
+            if not staged:
                 d = i
             wait_bytes(g1.at[:, 0:lanes], q_recv.at[d])
             first_lane = quad_at(d, -1) * lanes
@@ -494,6 +523,8 @@
     for_chunks(lambda i: first_sweep(i, (2, 3)))
     for_chunks(lambda i: second_sweep(i, (3,), (0,)))
     own_trace[...] = trace()
+    if staged:
+        pl.semaphore_wait(relay.at[1], 3)
     share_first()
 
     half = span // 2
@@ -582,7 +613,6 @@
     part2 = part2_own[...] + part2_got[...]
     is_first = n == 0
     part2 = jnp.where(is_first, part2, pltpu.roll(part2, CX - RX, 1))
-    part2_turned = jnp.transpose(jnp.broadcast_to(part2[0:1], (CX, CX)))[0:RX, 0:1]
 
     wait_bytes(part.at[0, 0:1, CX:], g_recv.at[4])
     wait_bytes(part.at[0, 0:1, :], g_recv.at[5])
@@ -661,15 +691,18 @@
 
     def against(block, row):
         return lax.dot_general(
+            jnp.broadcast_to(row, (BY, span)),
             block,
-            jnp.broadcast_to(row, (BY, span)),
             (((1,), (1,)), ((), ())),
             preferred_element_type=jnp.float32,
         )
 
     mine = opv[pl.ds(pl.multiple_of(n * RX, RX), RX), 0:span]
     last = against(mine, own_row) + against(op_other[...], other_row)
-    out_t[...] = part2_turned + last[:, 0:1]
+    row_t[...] = part2[0:1, 0:RX] + last[0:1, :]
+    store_t = pltpu.make_async_copy(row_t, out_t, o_local.at[3])
+    store_t.start()
+    stores.append(store_t)
 
     for own in stores:
         own.wait()
@@ -684,28 +717,45 @@
         wait_bytes(ref.at[0, 0:count, :], g_send.at[number + 1])
 
 
+def hand_over(pressure, traction, out_p, out_t, held_p, held_t, sem_in, sem_out):
+    parts = [(pressure.at[k, z], held_p.at[k, z], out_p.at[k, z]) for k in (0, 1) for z in (0, 1)]
+    parts.append((traction, held_t, out_t))
+    loads = [
+        pltpu.make_async_copy(src, held, sem_in.at[i]) for i, (src, held, _) in enumerate(parts)
+    ]
+    stores = [
+        pltpu.make_async_copy(held, dst, sem_out.at[i]) for i, (_, held, dst) in enumerate(parts)
+    ]
+    for load in loads:
+        load.start()
+    for load, store in zip(loads, stores):
+        load.wait()
+        store.start()
+    for store in stores:
+        store.wait()
+
+
 def local(forcing, material_ids, materials, boundary_operator):
     wide_count = lax.axis_size("wide")
     field = pltpu.VMEM((2, NZ, ROWS_ALL, CX), jnp.float32)
     gathered = pltpu.VMEM((BY, wide_count * CX), jnp.bfloat16)
     dma = pltpu.SemaphoreType.DMA
     anywhere = pl.BlockSpec(memory_space=pl.ANY)
-    hbm = pl.BlockSpec(memory_space=pltpu.HBM)
     rows = boundary_operator.shape[0]
     quads = wide_count // QUAD
-    return pl.pallas_call(
+    pressure, traction = pl.pallas_call(
         functools.partial(kernel, wide_count),
         out_shape=(
             jax.ShapeDtypeStruct(forcing.shape, jnp.float32),
-            jax.ShapeDtypeStruct((RX, 1), jnp.float32),
+            jax.ShapeDtypeStruct((1, RX), jnp.float32),
         ),
         in_specs=[
-            hbm,
-            hbm,
+            anywhere,
+            anywhere,
             pl.BlockSpec(memory_space=pltpu.SMEM),
-            hbm,
+            anywhere,
         ],
-        out_specs=(anywhere, pl.BlockSpec(memory_space=pltpu.VMEM)),
+        out_specs=(anywhere, anywhere),
         scratch_shapes=[
             pltpu.VMEM(forcing.shape, jnp.float32),
             pltpu.VMEM(material_ids.shape, jnp.int32),
@@ -730,6 +780,7 @@
             pltpu.VMEM((2, 8, wide_count * CX), jnp.float32),
             pltpu.VMEM((8, CX), jnp.float32),
             pltpu.VMEM((8, CX), jnp.float32),
+            pltpu.VMEM((1, RX), jnp.float32),
             pltpu.VMEM((RX, wide_count * CX), jnp.bfloat16),
             dma((3,)),
             dma((BY,)),
@@ -741,8 +792,9 @@
             dma((3,)),
             dma((3,)),
             dma((3,)),
-            dma((3,)),
+            dma((4,)),
             dma((quads,)),
+            pltpu.SemaphoreType.REGULAR((2,)),
         ],
         compiler_params=pltpu.CompilerParams(
             collective_id=0, has_side_effects=True, vmem_limit_bytes=62 * 1024 * 1024
@@ -753,6 +805,22 @@
             transcendentals=0,
         ),
     )(forcing, material_ids, materials, boundary_operator)
+    pressure, traction = pl.pallas_call(
+        hand_over,
+        out_shape=(
+            jax.ShapeDtypeStruct(pressure.shape, jnp.float32),
+            jax.ShapeDtypeStruct(traction.shape, jnp.float32),
+        ),
+        in_specs=[anywhere, anywhere],
+        out_specs=(anywhere, anywhere),
+        scratch_shapes=[
+            pltpu.VMEM(pressure.shape, jnp.float32),
+            pltpu.VMEM(traction.shape, jnp.float32),
+            dma((5,)),
+            dma((5,)),
+        ],
+    )(pressure, traction)
+    return pressure, traction.reshape(RX, 1)
 
 
 def solution(mesh):

time: 43.5 us -> 39.4 us (0.906)
  local copies, waits for them, and re-layouts: 3.11 us -> 0 us
  Pallas kernels: 39.5 us -> 38.6 us
    pallas_call x1, Pallas kernels: 39.5 us -> 36.8 us  [local(): pl.pallas_call(functools.partial(kernel, wide_count), out_shape=(jax.Shap...]
    unnamed x1 -> x0, local copies, waits for them, and re-layouts: 1.77 us -> none
    pallas_call x0 -> x1, Pallas kernels: none -> 1.76 us  [local(): pl.pallas_call(hand_over, out_shape=(jax.ShapeDtypeStruct(pressure.shape,...]
    pallas_call x1 -> x0, local copies, waits for them, and re-layouts: 1.34 us -> none  [local(): pl.pallas_call(functools.partial(kernel, wide_count), out_shape=(jax.Shap...]
where the time goes in v3:
time: 39.4 us; the launch traced here: 39.2 us
  Pallas kernels  38.6 us (98%)
  between operations  0.64 us (2%)
    pallas_call x1, Pallas kernels, local(): pl.pallas_call(functools.partial(kernel, wide_count), out_shape=(jax.Shap...  36.8 us
    pallas_call x1, Pallas kernels, local(): pl.pallas_call(hand_over, out_shape=(jax.ShapeDtypeStruct(pressure.shape,...  1.76 us

profile of v3, /device:TPU:1, one launch (start us, length us, event | category | flops | bytes accessed | tf_op | source)
XLA Modules:
  0.0 39.2 jit_solution(5687701587130103007)
XLA Ops:
  0.6 36.8 %shard_map.59 = (f32[2,2,192,128]{3,2,1,0:T(8,128)}, f32[1,64]{1,0:T(1,128)}) custom-call(f32[2,2,192,128]{3,2,1,0:T(8,128)} %forcing.1, s32[2,192,128]{2,1,0:T(8,128)} %ids.1, f32[8]{0:T(128)} %materials.1, bf16[128,65536]{1,0:T(8,128)(2,1)} %op.1), custom_call_target="tpu_custom_call" | custom-call | flops 33554432 | bytes 16777216 | tf_op jit(solution)/shard_map/pallas_call | solution.py:746
  37.5 1.8 %shard_map.60 = (f32[2,2,192,128]{3,2,1,0:T(8,128)}, f32[1,64]{1,0:T(1,128)}) custom-call(f32[2,2,192,128]{3,2,1,0:T(8,128)} %get-tuple-element.6.pressure, f32[1,64]{1,0:T(1,128)} %get-tuple-element.7.traction), custom_call_target="tpu_custom_call" | custom-call | tf_op jit(solution)/shard_map/pallas_call | solution.py:808

commit v4 on v3

--- a/solution.py
+++ b/solution.py
@@ -78,7 +78,9 @@
     coef,
     part2_own,
     part2_got,
+    swap,
     row_t,
+    op_mine,
     op_other,
     local_sem,
     op_sem,
@@ -93,6 +95,7 @@
     o_local,
     q_recv,
     relay,
+    pair_send,
 ):
     v = lax.axis_index("vol")
     w = lax.axis_index("wide")
@@ -125,35 +128,23 @@
             greet(v, side, narrow)
     greet(v, w, other_n)
 
-    quads = wide_count // QUAD
+    half_count = wide_count // 2
     my_quad, my_place = w // QUAD, lax.rem(w, QUAD)
-    staged = quads == 2 * QUAD
-
-    def quad_at(d, sign):
-        if not staged:
-            return lax.rem(my_quad + sign * d + quads, quads)
-        high, low = my_quad // QUAD, lax.rem(my_quad, QUAD)
-        high = lax.rem(high + d // QUAD, 2)
-        low = lax.rem(low + sign * lax.rem(d, QUAD) + QUAD, QUAD)
+    my_high, my_low = my_quad // QUAD, lax.rem(my_quad, QUAD)
+
+    def quad_at(d):
+        high = lax.rem(my_high + d // QUAD, 2)
+        low = lax.rem(my_low + lax.rem(d, QUAD), QUAD)
         return high * QUAD + low
 
     y_ring = [my_quad * QUAD + lax.rem(my_place + j, QUAD) for j in range(1, QUAD)]
-    if staged:
-        for j in range(1, QUAD):
-            greet(v, y_ring[j - 1], n)
-            greet(v, quad_at(j, 1) * QUAD + my_place, n)
-        opposite = lax.rem(w + wide_count // 2, wide_count)
-        greet(v, opposite, n)
-        greet(v, opposite, other_n)
-    else:
-
-        def greet_wide(j, carry):
-            for narrow in (n, other_n):
-                signal(barrier, v, lax.rem(w + j, wide_count), narrow)
-            return carry
-
-        lax.fori_loop(1, wide_count, greet_wide, 0)
-        greeted.extend([0] * (2 * (wide_count - 1)))
+    x_ring = [quad_at(j) * QUAD + my_place for j in range(1, QUAD)]
+    opposite = lax.rem(w + half_count, wide_count)
+    for vol in (v, other_v):
+        for wide in y_ring + x_ring:
+            greet(vol, wide, n)
+        greet(vol, opposite, n)
+        greet(vol, opposite, other_n)
 
     load_ids = pltpu.make_async_copy(ids, iv, local_sem.at[0])
     load_f = pltpu.make_async_copy(forcing, fv, local_sem.at[1])
@@ -184,9 +175,18 @@
 
     span = wide_count * CX
 
+    half = span // 2
+
     def op_chunk(s):
-        columns = pl.ds(pl.multiple_of(s * span, span), span)
-        return pltpu.make_async_copy(op.at[:, columns], opv.at[:, columns], op_sem.at[s])
+        return pltpu.make_async_copy(
+            op.at[:, pl.ds(pl.multiple_of(s * span + v * half, half), half)],
+            opv.at[:, pl.ds(pl.multiple_of(s * half, half), half)],
+            op_sem.at[s],
+        )
+
+    load_mine = pltpu.make_async_copy(
+        op.at[pl.ds(pl.multiple_of(n * RX, RX), RX), 0:span], op_mine, local_sem.at[3]
+    )
 
     edge_row = pl.multiple_of(other_n * (CY - 8), 8)
     lane = lax.broadcasted_iota(jnp.int32, (GROUP_ROWS, CX), 1)
@@ -215,9 +215,8 @@
         corner[k] = edge
 
     pl.semaphore_wait(barrier, len(greeted))
-    if staged:
-        for place in y_ring:
-            signal(relay.at[0], v, place, n)
+    for wide in y_ring:
+        signal(relay.at[0], v, wide, n)
 
     sends = []
 
@@ -283,10 +282,10 @@
         return carry
 
     lax.fori_loop(0, BY, start_op, 0)
-    if staged:
-        pl.semaphore_wait(relay.at[0], QUAD - 1)
-        for wide, narrow in ((opposite, n), (opposite, other_n), (w, other_n)):
-            signal(relay.at[1], v, wide, narrow)
+    load_mine.start()
+    pl.semaphore_wait(relay.at[0], QUAD - 1)
+    for wide, narrow in ((opposite, n), (opposite, other_n), (w, other_n)):
+        signal(relay.at[1], v, wide, narrow)
 
     def wait_bytes(ref, sem):
         pltpu.make_async_copy(ref, ref, sem).wait()
@@ -463,71 +462,78 @@
     def trace():
         return pb[0, NZ - 1, pl.ds(PAD, BY, stride=CY // BY), :].astype(jnp.bfloat16)
 
-    row16 = lax.broadcasted_iota(jnp.int32, (BY, CX), 0)
-
-    def product(g, low, high):
-        def add(s, total):
-            block = opv[:, pl.ds(pl.multiple_of(s * span, span), span)]
+    row_of = lax.rem(lax.broadcasted_iota(jnp.int32, (2 * BY, CX), 0), BY)
+
+    owner = my_high
+    elsewhere = owner != v
+    half_columns = pl.ds(pl.multiple_of(lax.rem(w, half_count) * CX, CX), CX)
+
+    def trace_copy(block, g, send_sem, recv_sem, wide):
+        return pltpu.make_async_remote_copy(
+            src_ref=block,
+            dst_ref=g.at[v, :, half_columns],
+            send_sem=send_sem,
+            recv_sem=recv_sem,
+            device_id=device(owner, wide, n),
+            device_id_type=MESH,
+        )
+
+    def share_trace(block, g, number, recv_sem):
+        def to(i, carry):
+            i = wide_count - i
+            place = lax.rem(my_place + lax.rem(i, QUAD), QUAD)
+            wide = quad_at(i // QUAD) * QUAD + place
+            trace_copy(block, g, g_send.at[number], recv_sem, wide).start()
+            return carry
+
+        lax.fori_loop(1, wide_count, to, 0)
+
+        @pl.when(elsewhere)
+        def _():
+            trace_copy(block, g, pair_send.at[number], recv_sem, w).start()
+
+        @pl.when(jnp.logical_not(elsewhere))
+        def _():
+            pltpu.make_async_copy(block, g.at[v, :, half_columns], recv_sem).start()
+
+    lanes = QUAD * CX
+
+    def against_quad(x, first_lane, total, first_row):
+        for s in range(first_row, BY):
+            block = opv[:, pl.ds(pl.multiple_of(s * half + first_lane, lanes), lanes)]
             rows = lax.dot_general(
-                g[...], block, (((1,), (1,)), ((), ())), preferred_element_type=jnp.float32
+                x, block, (((1,), (1,)), ((), ())), preferred_element_type=jnp.float32
             )
-            return total + jnp.where(row16 == s, rows, 0.0)
-
-        total = lax.fori_loop(
-            low, high, add, jnp.zeros((BY, CX), jnp.float32), unroll=5
-        )
-        return jnp.sum(total, axis=0, keepdims=True)
-
-    def share_first():
-        def to(i, carry):
-            d = i // QUAD
-            place = lax.rem(my_place + lax.rem(i, QUAD), QUAD)
-            pltpu.make_async_remote_copy(
-                src_ref=own_trace,
-                dst_ref=g1.at[:, my_columns],
-                send_sem=g_send.at[0],
-                recv_sem=q_recv.at[d],
-                device_id=device(v, quad_at(d, 1) * QUAD + place, n),
-                device_id_type=MESH,
-            ).start()
-            return carry
-
-        lax.fori_loop(1, wide_count, lambda i, carry: to(wide_count - i, carry), 0)
-        pltpu.make_async_copy(own_trace, g1.at[:, my_columns], q_recv.at[0]).start()
-
-    lanes = QUAD * CX
-
-    def product_first():
-        for s in range(BY):
-            op_chunk(s).wait()
-
+            total = total + jnp.where(row_of == s, rows, 0.0)
+        return total
+
+    def product(g, first_row, arriving):
         def add(i, total):
-            step = lax.rem(i, QUAD)
-            d = i - step + step + step // 2 - 2 * (step // 3)
-            if not staged:
-                d = i
-            wait_bytes(g1.at[:, 0:lanes], q_recv.at[d])
-            first_lane = quad_at(d, -1) * lanes
-            x = g1[:, pl.ds(pl.multiple_of(first_lane, lanes), lanes)]
-            for s in range(BY):
-                block = opv[:, pl.ds(pl.multiple_of(s * span + first_lane, lanes), lanes)]
-                rows = lax.dot_general(
-                    x, block, (((1,), (1,)), ((), ())), preferred_element_type=jnp.float32
-                )
-                total = total + jnp.where(row16 == s, rows, 0.0)
-            return total
-
-        total = lax.fori_loop(0, quads, add, jnp.zeros((BY, CX), jnp.float32))
-        return jnp.sum(total, axis=0, keepdims=True)
+            low = lax.rem(my_low + i + i // 2 - 2 * (i // 3), QUAD)
+            if arriving:
+                wait_bytes(g.at[:, :, 0:lanes], q_recv.at[low])
+            x = g[:, :, pl.ds(pl.multiple_of(low * lanes, lanes), lanes)]
+            return against_quad(x.reshape(2 * BY, lanes), low * lanes, total, first_row)
+
+        total = lax.fori_loop(0, QUAD, add, jnp.zeros((2 * BY, CX), jnp.float32))
+        return [
+            jnp.sum(total[k * BY : (k + 1) * BY], axis=0, keepdims=True) for k in (0, 1)
+        ]
+
+    is_low = v == 0
+
+    def mine_and_theirs(parts):
+        return (
+            jnp.where(is_low, parts[0], parts[1]),
+            jnp.where(is_low, parts[1], parts[0]),
+        )
 
     for_chunks(lambda i: first_sweep(i, (2, 3)))
     for_chunks(lambda i: second_sweep(i, (3,), (0,)))
-    own_trace[...] = trace()
-    if staged:
-        pl.semaphore_wait(relay.at[1], 3)
-    share_first()
-
-    half = span // 2
+    own_trace[0] = trace()
+    pl.semaphore_wait(relay.at[1], 3)
+    share_trace(own_trace.at[0], g1, 0, q_recv.at[my_low])
+
     my_half = pl.ds(pl.multiple_of(v * half, half), half)
     their_half = pl.ds(pl.multiple_of(other_v * half, half), half)
     send(
@@ -542,8 +548,8 @@
     for_chunks(lambda i: second_sweep(i, (1, 2, 3), both))
     for_chunks(lambda i: third_sweep(i, (2, 3)))
     for_chunks(lambda i: fourth_sweep(i, (3,)))
-    g2[:, my_columns] = trace()
-    share(g2.at[:, my_columns], (1,), (n,))
+    own_trace[1] = trace()
+    share_trace(own_trace.at[1], g2, 1, g_recv.at[1])
 
     top = NZ - 1
     lane1 = lax.broadcasted_iota(jnp.int32, (8, CX), 1)
@@ -571,7 +577,15 @@
     )
     share(coef.at[n, 0:4, my_columns], (2, 3), (n, other_n))
 
-    part[n, 0:1, my_columns] = product_first()
+    for s in range(BY):
+        op_chunk(s).wait()
+    mine1, theirs1 = mine_and_theirs(product(g1, 0, True))
+    swap[0] = jnp.broadcast_to(theirs1, (8, CX))
+    send(swap.at[0], swap.at[1], x_send.at[3], x_recv.at[3], device(other_v, w, n))
+    for_chunks(lambda i: second_sweep(i, (0,), both))
+    for_chunks(lambda i: third_sweep(i, (0, 1)))
+    wait_bytes(swap.at[1], x_recv.at[3])
+    part[n, 0:1, my_columns] = mine1 + swap[1, 0:1, :]
     share(part.at[n, 0:1, my_columns], (4, 5), (n, other_n))
 
     wait_bytes(op_other.at[:, my_half], x_recv.at[0])
@@ -582,11 +596,20 @@
         x_recv.at[1],
         device(other_v, w, n),
     )
-    wait_bytes(g2.at[:, CX:], g_recv.at[1])
-    part2_own[...] = jnp.broadcast_to(product(g2, 1, BY), (8, CX))
-    send(part2_own, part2_got, x_send.at[2], x_recv.at[2], device(v, w, other_n))
-    for_chunks(lambda i: second_sweep(i, (0,), both))
-    for_chunks(lambda i: third_sweep(i, (0, 1)))
+    wait_bytes(g2, g_recv.at[1])
+    mine2, theirs2 = mine_and_theirs(product(g2, 1, False))
+    part2_own[0] = jnp.broadcast_to(mine2, (8, CX))
+    part2_own[1] = jnp.broadcast_to(theirs2, (8, CX))
+    for number, (which, vol, narrow) in enumerate(
+        ((0, v, other_n), (1, other_v, n), (1, other_v, other_n))
+    ):
+        send(
+            part2_own.at[which],
+            part2_got.at[number],
+            x_send.at[4 + number],
+            x_recv.at[4 + number],
+            device(vol, w, narrow),
+        )
     for_chunks(lambda i: fourth_sweep(i, (0, 1, 2)))
 
     def store_rows(number, y, count):
@@ -609,8 +632,9 @@
     wait_bytes(coef.at[0, 0:4, CX:], g_recv.at[2])
     wait_bytes(coef.at[0, 0:4, :], g_recv.at[3])
     wait_bytes(op_other.at[:, their_half], x_recv.at[1])
-    wait_bytes(part2_got, x_recv.at[2])
-    part2 = part2_own[...] + part2_got[...]
+    for number in range(3):
+        wait_bytes(part2_got.at[number], x_recv.at[4 + number])
+    part2 = part2_own[0] + part2_got[0] + part2_got[1] + part2_got[2]
     is_first = n == 0
     part2 = jnp.where(is_first, part2, pltpu.roll(part2, CX - RX, 1))
 
@@ -697,8 +721,8 @@
             preferred_element_type=jnp.float32,
         )
 
-    mine = opv[pl.ds(pl.multiple_of(n * RX, RX), RX), 0:span]
-    last = against(mine, own_row) + against(op_other[...], other_row)
+    load_mine.wait()
+    last = against(op_mine[...], own_row) + against(op_other[...], other_row)
     row_t[...] = part2[0:1, 0:RX] + last[0:1, :]
     store_t = pltpu.make_async_copy(row_t, out_t, o_local.at[3])
     store_t.start()
@@ -711,7 +735,13 @@
     for copy in sends:
         copy.wait_send()
     for number, g in enumerate((g1, g2)):
-        wait_bytes(g.at[:, CX:], g_send.at[number])
+        wait_bytes(g.at[0, :, 0 : (half_count - 1) * CX], g_send.at[number])
+        wait_bytes(g.at[0], g_send.at[number])
+
+        @pl.when(elsewhere)
+        def _(number=number):
+            wait_bytes(own_trace.at[number], pair_send.at[number])
+
     for number, ref, count in ((2, coef, 4), (4, part, 1)):
         wait_bytes(ref.at[0, 0:count, CX:], g_send.at[number])
         wait_bytes(ref.at[0, 0:count, :], g_send.at[number + 1])
@@ -738,11 +768,10 @@
 def local(forcing, material_ids, materials, boundary_operator):
     wide_count = lax.axis_size("wide")
     field = pltpu.VMEM((2, NZ, ROWS_ALL, CX), jnp.float32)
-    gathered = pltpu.VMEM((BY, wide_count * CX), jnp.bfloat16)
+    gathered = pltpu.VMEM((2, BY, wide_count * CX // 2), jnp.bfloat16)
     dma = pltpu.SemaphoreType.DMA
     anywhere = pl.BlockSpec(memory_space=pl.ANY)
     rows = boundary_operator.shape[0]
-    quads = wide_count // QUAD
     pressure, traction = pl.pallas_call(
         functools.partial(kernel, wide_count),
         out_shape=(
@@ -771,30 +800,33 @@
             pltpu.VMEM((2, 8, CX), jnp.float32),
             pltpu.VMEM((2, 2, GROUP_ROWS, CX), jnp.float32),
             pltpu.VMEM((2, 2, 8, CX), jnp.float32),
-            pltpu.VMEM(boundary_operator.shape, jnp.bfloat16),
-            pltpu.VMEM((BY, CX), jnp.bfloat16),
+            pltpu.VMEM((rows, boundary_operator.shape[1] // 2), jnp.bfloat16),
+            pltpu.VMEM((2, BY, CX), jnp.bfloat16),
             gathered,
             gathered,
             pltpu.VMEM((2, 8, wide_count * CX), jnp.float32),
             pltpu.VMEM((8, wide_count * CX), jnp.float32),
             pltpu.VMEM((2, 8, wide_count * CX), jnp.float32),
-            pltpu.VMEM((8, CX), jnp.float32),
-            pltpu.VMEM((8, CX), jnp.float32),
+            pltpu.VMEM((2, 8, CX), jnp.float32),
+            pltpu.VMEM((3, 8, CX), jnp.float32),
+            pltpu.VMEM((2, 8, CX), jnp.float32),
             pltpu.VMEM((1, RX), jnp.float32),
             pltpu.VMEM((RX, wide_count * CX), jnp.bfloat16),
-            dma((3,)),
+            pltpu.VMEM((RX, wide_count * CX), jnp.bfloat16),
+            dma((4,)),
             dma((BY,)),
             dma((14,)),
             dma((14,)),
             dma((6,)),
             dma((6,)),
-            dma((3,)),
-            dma((3,)),
+            dma((7,)),
+            dma((7,)),
             dma((3,)),
             dma((3,)),
             dma((4,)),
-            dma((quads,)),
+            dma((QUAD,)),
             pltpu.SemaphoreType.REGULAR((2,)),
+            dma((2,)),
         ],
         compiler_params=pltpu.CompilerParams(
             collective_id=0, has_side_effects=True, vmem_limit_bytes=62 * 1024 * 1024

time: 39.4 us -> 37.7 us (0.957)
  Pallas kernels: 38.6 us -> 36.9 us
    pallas_call x1, Pallas kernels: 36.8 us -> 35.1 us  [local(): pl.pallas_call(functools.partial(kernel, wide_count), out_shape=(jax.Shap...]
where the time goes in v4:
time: 37.7 us; the launch traced here: 37.5 us
  Pallas kernels  36.9 us (98%)
  between operations  0.64 us (2%)
    pallas_call x1, Pallas kernels, local(): pl.pallas_call(functools.partial(kernel, wide_count), out_shape=(jax.Shap...  35.1 us
    pallas_call x1, Pallas kernels, local(): pl.pallas_call(hand_over, out_shape=(jax.ShapeDtypeStruct(pressure.shape,...  1.76 us

profile of v4, /device:TPU:1, one launch (start us, length us, event | category | flops | bytes accessed | tf_op | source)
XLA Modules:
  0.0 37.5 jit_solution(15871503380926212750)
XLA Ops:
  0.6 35.1 %shard_map.59 = (f32[2,2,192,128]{3,2,1,0:T(8,128)}, f32[1,64]{1,0:T(1,128)}) custom-call(f32[2,2,192,128]{3,2,1,0:T(8,128)} %forcing.1, s32[2,192,128]{2,1,0:T(8,128)} %ids.1, f32[8]{0:T(128)} %materials.1, bf16[128,65536]{1,0:T(8,128)(2,1)} %op.1), custom_call_target="tpu_custom_call" | custom-call | flops 33554432 | bytes 16777216 | tf_op jit(solution)/shard_map/pallas_call | solution.py:775
  35.7 1.8 %shard_map.60 = (f32[2,2,192,128]{3,2,1,0:T(8,128)}, f32[1,64]{1,0:T(1,128)}) custom-call(f32[2,2,192,128]{3,2,1,0:T(8,128)} %get-tuple-element.6.pressure, f32[1,64]{1,0:T(1,128)} %get-tuple-element.7.traction), custom_call_target="tpu_custom_call" | custom-call | tf_op jit(solution)/shard_map/pallas_call | solution.py:840

commit v5 on v4

--- a/solution.py
+++ b/solution.py
@@ -121,11 +121,18 @@
         signal(barrier, vol, wide, narrow)
         greeted.append(0)
 
-    for narrow in (n, other_n):
-        for side in (left, w, right):
-            greet(other_v, side, narrow)
-        for side in (left, right):
-            greet(v, side, narrow)
+    has_left = w > 0
+    has_right = w < wide_count - 1
+    for has_side, side in ((has_left, left), (has_right, right)):
+
+        @pl.when(has_side)
+        def _(side=side):
+            for vol in (v, other_v):
+                for narrow in (n, other_n):
+                    signal(barrier, vol, side, narrow)
+
+    greet(other_v, w, n)
+    greet(other_v, w, other_n)
     greet(v, w, other_n)
 
     half_count = wide_count // 2
@@ -191,6 +198,15 @@
     edge_row = pl.multiple_of(other_n * (CY - 8), 8)
     lane = lax.broadcasted_iota(jnp.int32, (GROUP_ROWS, CX), 1)
     lane8 = lax.broadcasted_iota(jnp.int32, (8, CX), 1)
+    early = lax.rem(lane[: GROUP_ROWS // 2], SLOT) < 4
+    for direction, has_side in ((0, has_left), (1, has_right)):
+
+        @pl.when(jnp.logical_not(has_side))
+        def _(direction=direction):
+            for vol in (0, 1):
+                got_strip[direction, vol] = jnp.zeros((GROUP_ROWS // 2, CX), jnp.float32)
+                got_corner[direction, vol] = zeros8
+
     for k in (0, 1):
         packed = jnp.zeros((GROUP_ROWS, CX), jnp.float32)
         edge = jnp.zeros((8, CX), jnp.float32)
@@ -211,16 +227,19 @@
             at = field * SLOT
             x = pltpu.roll(x, at + 4, 1)
             edge = jnp.where((lane8 >= at) & (lane8 < at + SLOT), x, edge)
-        strip[k] = packed
+        a, b = packed[: GROUP_ROWS // 2], packed[GROUP_ROWS // 2 :]
+        strip[k, 0] = jnp.where(early, a, pltpu.roll(b, 4, 1))
+        strip[k, 1] = jnp.where(early, pltpu.roll(a, CX - 4, 1), b)
         corner[k] = edge
 
-    pl.semaphore_wait(barrier, len(greeted))
+    sides = jnp.where(has_left, 4, 0) + jnp.where(has_right, 4, 0)
+    pl.semaphore_wait(barrier, len(greeted) + sides)
     for wide in y_ring:
         signal(relay.at[0], v, wide, n)
 
     sends = []
 
-    def send(src, dst, send_sem, recv_sem, where):
+    def send(src, dst, send_sem, recv_sem, where, only=None):
         copy = pltpu.make_async_remote_copy(
             src_ref=src,
             dst_ref=dst,
@@ -229,20 +248,27 @@
             device_id=where,
             device_id_type=MESH,
         )
-        copy.start()
-        sends.append(copy)
-        return copy
+        if only is None:
+            copy.start()
+        else:
+
+            @pl.when(only)
+            def _():
+                copy.start()
+
+        sends.append((copy, only))
 
     own_layers = pl.ds(2 * v, 2)
     there_row = pl.multiple_of(PAD - HALO + n * (CY + HALO), 8)
     for k in (0, 1):
-        for direction, side in ((0, right), (1, left)):
+        for direction, side, has_side in ((0, right, has_right), (1, left, has_left)):
             send(
-                strip.at[k],
+                strip.at[k, direction],
                 got_strip.at[direction, v],
                 s_send.at[6 + 2 * direction + k],
                 s_recv.at[6 + 2 * direction + v],
                 device(k, side, n),
+                has_side,
             )
     send(
         fv.at[other_v],
@@ -268,13 +294,14 @@
             s_recv.at[4 + v],
             device(k, w, other_n),
         )
-        for direction, side in ((0, right), (1, left)):
+        for direction, side, has_side in ((0, right, has_right), (1, left, has_left)):
             send(
                 corner.at[k],
                 got_corner.at[direction, v],
                 s_send.at[10 + 2 * direction + k],
                 s_recv.at[10 + 2 * direction + v],
                 device(k, side, other_n),
+                has_side,
             )
 
     def start_op(s, carry):
@@ -290,24 +317,26 @@
     def wait_bytes(ref, sem):
         pltpu.make_async_copy(ref, ref, sem).wait()
 
-    has_left = w > 0
-    has_right = w < wide_count - 1
-    for direction in (0, 1):
-        for vol in (0, 1):
-            wait_bytes(got_strip.at[direction, vol], s_recv.at[6 + 2 * direction + vol])
-            wait_bytes(got_corner.at[direction, vol], s_recv.at[10 + 2 * direction + vol])
-    keep_left = jnp.where(has_left, 1.0, 0.0)
-    keep_right = jnp.where(has_right, 1.0, 0.0)
+    for direction, has_side in ((0, has_left), (1, has_right)):
+
+        @pl.when(has_side)
+        def _(direction=direction):
+            for vol in (0, 1):
+                wait_bytes(got_strip.at[direction, vol], s_recv.at[6 + 2 * direction + vol])
+                wait_bytes(got_corner.at[direction, vol], s_recv.at[10 + 2 * direction + vol])
+
     for z in range(NZ):
         vol = z // 2
-        from_left = lax.rem(lane, SLOT) < 4
-        merged = jnp.where(
-            from_left, got_strip[0, vol] * keep_left, got_strip[1, vol] * keep_right
+        a, b = got_strip[0, vol], got_strip[1, vol]
+        merged = jnp.concatenate(
+            [
+                jnp.where(early, a, pltpu.roll(b, 4, 1)),
+                jnp.where(early, pltpu.roll(a, CX - 4, 1), b),
+            ],
+            axis=0,
         )
         from_left8 = lax.rem(lane8, SLOT) < 4
-        merged8 = jnp.where(
-            from_left8, got_corner[0, vol] * keep_left, got_corner[1, vol] * keep_right
-        )
+        merged8 = jnp.where(from_left8, got_corner[0, vol], got_corner[1, vol])
         for which, ref in ((0, f), (2, c)):
             field = which + z % 2
             for group in range(GROUPS):
@@ -551,6 +580,11 @@
     own_trace[1] = trace()
     share_trace(own_trace.at[1], g2, 1, g_recv.at[1])
 
+    for s in range(BY):
+        op_chunk(s).wait()
+    mine1, theirs1 = mine_and_theirs(product(g1, 0, True))
+    swap[0] = jnp.broadcast_to(theirs1, (8, CX))
+    send(swap.at[0], swap.at[1], x_send.at[3], x_recv.at[3], device(other_v, w, n))
     top = NZ - 1
     lane1 = lax.broadcasted_iota(jnp.int32, (8, CX), 1)
 
@@ -577,13 +611,6 @@
     )
     share(coef.at[n, 0:4, my_columns], (2, 3), (n, other_n))
 
-    for s in range(BY):
-        op_chunk(s).wait()
-    mine1, theirs1 = mine_and_theirs(product(g1, 0, True))
-    swap[0] = jnp.broadcast_to(theirs1, (8, CX))
-    send(swap.at[0], swap.at[1], x_send.at[3], x_recv.at[3], device(other_v, w, n))
-    for_chunks(lambda i: second_sweep(i, (0,), both))
-    for_chunks(lambda i: third_sweep(i, (0, 1)))
     wait_bytes(swap.at[1], x_recv.at[3])
     part[n, 0:1, my_columns] = mine1 + swap[1, 0:1, :]
     share(part.at[n, 0:1, my_columns], (4, 5), (n, other_n))
@@ -596,6 +623,27 @@
         x_recv.at[1],
         device(other_v, w, n),
     )
+    for_chunks(lambda i: second_sweep(i, (0,), both))
+    for_chunks(lambda i: third_sweep(i, (0, 1)))
+    for_chunks(lambda i: fourth_sweep(i, (0, 1, 2)))
+
+    def store_rows(number, y, count):
+        here = out_p.at[v, :, pl.ds(y, count), :]
+        own = pltpu.make_async_copy(
+            pb.at[0, own_layers, pl.ds(PAD + y, count), :], here, o_local.at[number]
+        )
+        own.start()
+        send(
+            pb.at[0, pl.ds(2 * other_v, 2), pl.ds(PAD + y, count), :],
+            here,
+            o_send.at[number],
+            o_recv.at[number],
+            device(other_v, w, n),
+        )
+        return own
+
+    stores = [store_rows(0, 8, CY - 16)]
+
     wait_bytes(g2, g_recv.at[1])
     mine2, theirs2 = mine_and_theirs(product(g2, 1, False))
     part2_own[0] = jnp.broadcast_to(mine2, (8, CX))
@@ -610,38 +658,14 @@
             x_recv.at[4 + number],
             device(vol, w, narrow),
         )
-    for_chunks(lambda i: fourth_sweep(i, (0, 1, 2)))
-
-    def store_rows(number, y, count):
-        here = out_p.at[v, :, pl.ds(y, count), :]
-        own = pltpu.make_async_copy(
-            pb.at[0, own_layers, pl.ds(PAD + y, count), :], here, o_local.at[number]
-        )
-        own.start()
-        send(
-            pb.at[0, pl.ds(2 * other_v, 2), pl.ds(PAD + y, count), :],
-            here,
-            o_send.at[number],
-            o_recv.at[number],
-            device(other_v, w, n),
-        )
-        return own
-
-    stores = [store_rows(0, 8, CY - 16)]
-
     wait_bytes(coef.at[0, 0:4, CX:], g_recv.at[2])
     wait_bytes(coef.at[0, 0:4, :], g_recv.at[3])
     wait_bytes(op_other.at[:, their_half], x_recv.at[1])
-    for number in range(3):
-        wait_bytes(part2_got.at[number], x_recv.at[4 + number])
-    part2 = part2_own[0] + part2_got[0] + part2_got[1] + part2_got[2]
-    is_first = n == 0
-    part2 = jnp.where(is_first, part2, pltpu.roll(part2, CX - RX, 1))
-
     wait_bytes(part.at[0, 0:1, CX:], g_recv.at[4])
     wait_bytes(part.at[0, 0:1, :], g_recv.at[5])
     total[0:1, :] = part[0, 0:1, :] + part[1, 0:1, :]
 
+    is_first = n == 0
     row8 = lax.broadcasted_iota(jnp.int32, (8, CX), 0)
     here = jnp.broadcast_to(total[0:1, my_columns], (8, CX))
     beyond = jnp.broadcast_to(
@@ -723,6 +747,10 @@
 
     load_mine.wait()
     last = against(op_mine[...], own_row) + against(op_other[...], other_row)
+    for number in range(3):
+        wait_bytes(part2_got.at[number], x_recv.at[4 + number])
+    part2 = part2_own[0] + part2_got[0] + part2_got[1] + part2_got[2]
+    part2 = jnp.where(is_first, part2, pltpu.roll(part2, CX - RX, 1))
     row_t[...] = part2[0:1, 0:RX] + last[0:1, :]
     store_t = pltpu.make_async_copy(row_t, out_t, o_local.at[3])
     store_t.start()
@@ -732,8 +760,15 @@
         own.wait()
     for number, (y, count) in enumerate(((8, CY - 16), (0, 8), (CY - 8, 8))):
         wait_bytes(out_p.at[other_v, :, pl.ds(y, count), :], o_recv.at[number])
-    for copy in sends:
-        copy.wait_send()
+    for copy, only in sends:
+        if only is None:
+            copy.wait_send()
+        else:
+
+            @pl.when(only)
+            def _(copy=copy):
+                copy.wait_send()
+
     for number, g in enumerate((g1, g2)):
         wait_bytes(g.at[0, :, 0 : (half_count - 1) * CX], g_send.at[number])
         wait_bytes(g.at[0], g_send.at[number])
@@ -796,9 +831,9 @@
             field,
             field,
             field,
-            pltpu.VMEM((2, GROUP_ROWS, CX), jnp.float32),
+            pltpu.VMEM((2, 2, GROUP_ROWS // 2, CX), jnp.float32),
             pltpu.VMEM((2, 8, CX), jnp.float32),
-            pltpu.VMEM((2, 2, GROUP_ROWS, CX), jnp.float32),
+            pltpu.VMEM((2, 2, GROUP_ROWS // 2, CX), jnp.float32),
             pltpu.VMEM((2, 2, 8, CX), jnp.float32),
             pltpu.VMEM((rows, boundary_operator.shape[1] // 2), jnp.bfloat16),
             pltpu.VMEM((2, BY, CX), jnp.bfloat16),

time: 37.7 us -> 35.7 us (0.947)
  Pallas kernels: 36.9 us -> 34.9 us
    pallas_call x1, Pallas kernels: 35.1 us -> 33.2 us  [local(): pl.pallas_call(functools.partial(kernel, wide_count), out_shape=(jax.Shap...]
where the time goes in v5:
time: 35.7 us; the launch traced here: 35.6 us
  Pallas kernels  34.9 us (98%)
  between operations  0.64 us (2%)
    pallas_call x1, Pallas kernels, local(): pl.pallas_call(functools.partial(kernel, wide_count), out_shape=(jax.Shap...  33.2 us
    pallas_call x1, Pallas kernels, local(): pl.pallas_call(hand_over, out_shape=(jax.ShapeDtypeStruct(pressure.shape,...  1.76 us

profile of v5, /device:TPU:1, one launch (start us, length us, event | category | flops | bytes accessed | tf_op | source)
XLA Modules:
  0.0 35.6 jit_solution(6695822627175056984)
XLA Ops:
  0.6 33.2 %shard_map.59 = (f32[2,2,192,128]{3,2,1,0:T(8,128)}, f32[1,64]{1,0:T(1,128)}) custom-call(f32[2,2,192,128]{3,2,1,0:T(8,128)} %forcing.1, s32[2,192,128]{2,1,0:T(8,128)} %ids.1, f32[8]{0:T(128)} %materials.1, bf16[128,65536]{1,0:T(8,128)(2,1)} %op.1), custom_call_target="tpu_custom_call" | custom-call | flops 33554432 | bytes 16777216 | tf_op jit(solution)/shard_map/pallas_call | solution.py:810
  33.8 1.8 %shard_map.60 = (f32[2,2,192,128]{3,2,1,0:T(8,128)}, f32[1,64]{1,0:T(1,128)}) custom-call(f32[2,2,192,128]{3,2,1,0:T(8,128)} %get-tuple-element.6.pressure, f32[1,64]{1,0:T(1,128)} %get-tuple-element.7.traction), custom_call_target="tpu_custom_call" | custom-call | tf_op jit(solution)/shard_map/pallas_call | solution.py:875

commit v6 on v5

--- a/solution.py
+++ b/solution.py
@@ -477,7 +477,7 @@
                 ).start()
             return carry
 
-        lax.fori_loop(0, wide_count - 1, to, 0)
+        lax.fori_loop(0, wide_count - 1, to, 0, unroll=wide_count - 1)
         if len(numbers) == 2:
             pltpu.make_async_remote_copy(
                 src_ref=block,
@@ -515,7 +515,7 @@
             trace_copy(block, g, g_send.at[number], recv_sem, wide).start()
             return carry
 
-        lax.fori_loop(1, wide_count, to, 0)
+        lax.fori_loop(1, wide_count, to, 0, unroll=wide_count - 1)
 
         @pl.when(elsewhere)
         def _():

time: 35.7 us -> 35 us (0.980)
  Pallas kernels: 34.9 us -> 34.2 us
    pallas_call x1, Pallas kernels: 33.2 us -> 32.4 us  [local(): pl.pallas_call(functools.partial(kernel, wide_count), out_shape=(jax.Shap...]
where the time goes in v6:
time: 35 us; the launch traced here: 34.8 us
  Pallas kernels  34.2 us (98%)
  between operations  0.64 us (2%)
    pallas_call x1, Pallas kernels, local(): pl.pallas_call(functools.partial(kernel, wide_count), out_shape=(jax.Shap...  32.4 us
    pallas_call x1, Pallas kernels, local(): pl.pallas_call(hand_over, out_shape=(jax.ShapeDtypeStruct(pressure.shape,...  1.76 us

profile of v6, /device:TPU:1, one launch (start us, length us, event | category | flops | bytes accessed | tf_op | source)
XLA Modules:
  0.0 34.8 jit_solution(13254080813407047817)
XLA Ops:
  0.6 32.4 %shard_map.59 = (f32[2,2,192,128]{3,2,1,0:T(8,128)}, f32[1,64]{1,0:T(1,128)}) custom-call(f32[2,2,192,128]{3,2,1,0:T(8,128)} %forcing.1, s32[2,192,128]{2,1,0:T(8,128)} %ids.1, f32[8]{0:T(128)} %materials.1, bf16[128,65536]{1,0:T(8,128)(2,1)} %op.1), custom_call_target="tpu_custom_call" | custom-call | flops 33554432 | bytes 16777216 | tf_op jit(solution)/shard_map/pallas_call | solution.py:810
  33.1 1.8 %shard_map.60 = (f32[2,2,192,128]{3,2,1,0:T(8,128)}, f32[1,64]{1,0:T(1,128)}) custom-call(f32[2,2,192,128]{3,2,1,0:T(8,128)} %get-tuple-element.6.pressure, f32[1,64]{1,0:T(1,128)} %get-tuple-element.7.traction), custom_call_target="tpu_custom_call" | custom-call | tf_op jit(solution)/shard_map/pallas_call | solution.py:875

commit v7 on v6

--- a/solution.py
+++ b/solution.py
@@ -544,7 +544,9 @@
             x = g[:, :, pl.ds(pl.multiple_of(low * lanes, lanes), lanes)]
             return against_quad(x.reshape(2 * BY, lanes), low * lanes, total, first_row)
 
-        total = lax.fori_loop(0, QUAD, add, jnp.zeros((2 * BY, CX), jnp.float32))
+        total = lax.fori_loop(
+            0, QUAD, add, jnp.zeros((2 * BY, CX), jnp.float32), unroll=QUAD
+        )
         return [
             jnp.sum(total[k * BY : (k + 1) * BY], axis=0, keepdims=True) for k in (0, 1)
         ]
@@ -574,7 +576,7 @@
     )
 
     for_chunks(lambda i: first_sweep(i, (0, 1)))
-    for_chunks(lambda i: second_sweep(i, (1, 2, 3), both))
+    for_chunks(lambda i: (second_sweep(i, (1, 2), both), second_sweep(i, (3,), (1,))))
     for_chunks(lambda i: third_sweep(i, (2, 3)))
     for_chunks(lambda i: fourth_sweep(i, (3,)))
     own_trace[1] = trace()

time: 35 us -> 35.1 us (level)
  no operation moved by 1% of the time
where the time goes in v7:
time: 35.1 us; the launch traced here: 34.9 us
  Pallas kernels  34.3 us (98%)
  between operations  0.64 us (2%)
    pallas_call x1, Pallas kernels, local(): pl.pallas_call(functools.partial(kernel, wide_count), out_shape=(jax.Shap...  32.5 us
    pallas_call x1, Pallas kernels, local(): pl.pallas_call(hand_over, out_shape=(jax.ShapeDtypeStruct(pressure.shape,...  1.76 us

profile of v7, /device:TPU:1, one launch (start us, length us, event | category | flops | bytes accessed | tf_op | source)
XLA Modules:
  0.0 34.9 jit_solution(7466845900121035292)
XLA Ops:
  0.6 32.5 %shard_map.59 = (f32[2,2,192,128]{3,2,1,0:T(8,128)}, f32[1,64]{1,0:T(1,128)}) custom-call(f32[2,2,192,128]{3,2,1,0:T(8,128)} %forcing.1, s32[2,192,128]{2,1,0:T(8,128)} %ids.1, f32[8]{0:T(128)} %materials.1, bf16[128,65536]{1,0:T(8,128)(2,1)} %op.1), custom_call_target="tpu_custom_call" | custom-call | flops 33554432 | bytes 16777216 | tf_op jit(solution)/shard_map/pallas_call | solution.py:812
  33.2 1.8 %shard_map.60 = (f32[2,2,192,128]{3,2,1,0:T(8,128)}, f32[1,64]{1,0:T(1,128)}) custom-call(f32[2,2,192,128]{3,2,1,0:T(8,128)} %get-tuple-element.6.pressure, f32[1,64]{1,0:T(1,128)} %get-tuple-element.7.traction), custom_call_target="tpu_custom_call" | custom-call | tf_op jit(solution)/shard_map/pallas_call | solution.py:877
